TPU v7x, 256 devices: a whole 4x4x8 slice. The times are simulated.
256 devices in a mesh: pipe: 2 (over core), expert: 32 (over z, x), dp: 4 (over y).
Axes of the slice: x: 4, y: 4, z: 8, core: 2. Of those that a mesh axis runs over, the one named last changes fastest.
Arguments:
- layer_input: bfloat16 [2, 16384, 4096], P('pipe', ('expert', 'dp')), may hold values from -6 to 6
- out_grad: bfloat16 [2, 16384, 4096], P('pipe', ('expert', 'dp')), may hold values from -2 to 2
- routes: int32 [2, 16384, 1], P('pipe', ('expert', 'dp')), may hold values from 0 to 15; in each aligned block of 128 rows (0 to 127, 128 to 255, ..., all dimensions but the last counted through in order) at most 16 rows name the same one
- gates: float32 [2, 16384], P('pipe', ('expert', 'dp')), may hold values from 0.2 to 1
- w_gate: bfloat16 [2, 4096, 12288], P('pipe', 'dp', 'expert'), may hold values from -0.09375 to 0.09375
- w_up: bfloat16 [2, 4096, 12288], P('pipe', 'dp', 'expert'), may hold values from -0.09375 to 0.09375
- w_down: bfloat16 [2, 4096, 12288], P('pipe', 'dp', 'expert'), may hold values from -0.21875 to 0.21875
Outputs:
- passed_grad: bfloat16 [2, 16384, 4096], P('pipe', ('expert', 'dp'))
- grad_gate: float32 [2, 4096, 12288], P('pipe', 'dp', 'expert')
- grad_up: float32 [2, 4096, 12288], P('pipe', 'dp', 'expert')
- grad_down: float32 [2, 4096, 12288], P('pipe', 'dp', 'expert')
Inputs may be any that keep to these rules, and one draw needn't show every extreme that they name: `routes`: among the 128 tokens of one device, at most 16 have the same expert.
All inputs are finite; a program needn't handle non-finite values.
Results may differ from a plain program's by a relative error of at most 0.012.
Values may be sent and summed in bfloat16 or wider, within the bound.
No kernel may reach another device: no remote copies, remote signals or barrier semaphores. Data moves between devices by JAX's collectives and lax.ppermute only.
A program may use at most 128 MiB of HBM per device.

v0:
```python
import functools

import jax
import jax.numpy as jnp
from jax import lax
from jax.experimental import pallas as pl
from jax.experimental.pallas import tpu as pltpu
from jax.sharding import PartitionSpec as P

F32, BF16 = jnp.float32, jnp.bfloat16
OUTER = (((0,), (0,)), ((), ()))
INNER = (((1,), (1,)), ((), ()))
VMEM_BYTES = 56 * 2**20


def along_z(i, step, zs, xs):
    return (i // xs + step) % zs * xs + i % xs


def to_mate(i, xs):
    return i ^ 1


def to_other(i, xs):
    x = i % xs
    return i - x + (x + (1 if x % 2 else -1)) % xs


def to_diagonal(i, xs):
    x = i % xs
    return i - x + (x + 2) % xs


def moved(block, place):
    return lax.ppermute(block, "expert", [(i, place(i)) for i in range(lax.axis_size("expert"))])


def after(value, *earlier):
    return lax.optimization_barrier((value,) + earlier)[0]


def activations(gate_pre, up_pre, d_hidden):
    sigmoid_gate = jax.nn.sigmoid(gate_pre)
    silu_gate = gate_pre * sigmoid_gate
    hidden = (silu_gate * up_pre).astype(BF16)
    d_up = (d_hidden * silu_gate).astype(BF16)
    d_gate = (d_hidden * up_pre * sigmoid_gate * (1.0 + gate_pre * (1.0 - sigmoid_gate))).astype(BF16)
    return hidden, d_gate, d_up


def expert_kernel(counts, capacity, *refs):
    pieces, refs = refs[:len(counts)], refs[len(counts):]
    weights, out_x, out_dy, hidden, slopes, flat_x, flat_dy, sums, held, arrived, loaded, kept = refs
    width, half = flat_x.shape[1], hidden.shape[1]
    halves, cut = 2, 1024
    wide = width // halves
    loads = [
        pltpu.make_async_copy(
            weights.at[:, pl.ds(c * cut, cut), :], held.at[:, pl.ds(c * cut, cut), :], loaded.at[c]
        )
        for c in range(width // cut)
    ]
    for h in range(halves):
        columns = pl.ds(h * wide, wide)
        at = 0
        for piece, count in zip(pieces, counts):
            rows = count * capacity
            for part, flat in enumerate((flat_x, flat_dy)):
                pltpu.make_async_copy(
                    piece.at[pl.ds(part * rows, rows), columns],
                    flat.at[pl.ds(at, rows), columns],
                    arrived.at[part, h],
                ).start()
            at += rows
        for c in range(h * wide // cut, (h + 1) * wide // cut):
            loads[c].start()
    sums[...] = jnp.zeros_like(sums)
    keeps = []
    for h in range(halves):
        columns = pl.ds(h * wide, wide)
        for part, (flat, out) in enumerate(((flat_x, out_x), (flat_dy, out_dy))):
            whole = flat.at[:, columns]
            pltpu.make_async_copy(whole, whole, arrived.at[part, h]).wait()
            keep = pltpu.make_async_copy(whole, out.at[:, columns], kept.at[part, h])
            keep.start()
            keeps.append(keep)
        for c in range(h * wide // cut, (h + 1) * wide // cut):
            loads[c].wait()
            here = pl.ds(c * cut, cut)
            x, dy = flat_x[:, here], flat_dy[:, here]
            sums[0] += jnp.dot(x, held[0, here, :], preferred_element_type=F32)
            sums[1] += jnp.dot(x, held[1, here, :], preferred_element_type=F32)
            sums[2] += jnp.dot(dy, held[2, here, :], preferred_element_type=F32)

    hidden[...], slopes[:, :half], slopes[:, half:] = activations(sums[0], sums[1], sums[2])
    for keep in keeps:
        keep.wait()


def expert_block(pieces, weights, capacity):
    counts = [p.shape[0] // (2 * capacity) for p in pieces]
    rows = sum(counts) * capacity
    width, half = weights.shape[1:]
    anywhere, whole = pl.BlockSpec(memory_space=pl.ANY), pl.BlockSpec()
    return pl.pallas_call(
        functools.partial(expert_kernel, counts, capacity),
        in_specs=[anywhere] * (len(pieces) + 1),
        out_specs=[anywhere, anywhere, whole, whole],
        out_shape=[
            jax.ShapeDtypeStruct((rows, width), BF16),
            jax.ShapeDtypeStruct((rows, width), BF16),
            jax.ShapeDtypeStruct((rows, half), BF16),
            jax.ShapeDtypeStruct((rows, 2 * half), BF16),
        ],
        scratch_shapes=[
            pltpu.VMEM((rows, width), BF16),
            pltpu.VMEM((rows, width), BF16),
            pltpu.VMEM((3, rows, half), F32),
            pltpu.VMEM(weights.shape, BF16),
            pltpu.SemaphoreType.DMA((2, 2)),
            pltpu.SemaphoreType.DMA((width // 1024,)),
            pltpu.SemaphoreType.DMA((2, 2)),
        ],
        compiler_params=pltpu.CompilerParams(vmem_limit_bytes=VMEM_BYTES),
        cost_estimate=pl.CostEstimate(
            flops=6 * rows * width * half, bytes_accessed=20 * 2**20, transcendentals=rows * half
        ),
    )(*pieces, weights)


def back_kernel(slopes, weights, *backs):
    half = weights.shape[2]
    value = lax.dot_general(slopes[:, :half], weights[0], INNER, preferred_element_type=F32)
    value += lax.dot_general(slopes[:, half:], weights[1], INNER, preferred_element_type=F32)
    value = value.astype(BF16)
    rows = slopes.shape[0] // 4
    for i, back in enumerate(backs):
        back[...] = value[i * rows:(i + 1) * rows]


def back_block(slopes, weights):
    rows, (width, half), cut = slopes.shape[0], weights.shape[1:], 1024
    return pl.pallas_call(
        back_kernel,
        grid=(width // cut,),
        in_specs=[
            pl.BlockSpec((rows, 2 * half), lambda k: (0, 0)),
            pl.BlockSpec((2, cut, half), lambda k: (0, k, 0)),
        ],
        out_specs=[pl.BlockSpec((rows // 4, cut), lambda k: (0, k))] * 4,
        out_shape=[jax.ShapeDtypeStruct((rows // 4, width), BF16)] * 4,
        compiler_params=pltpu.CompilerParams(vmem_limit_bytes=VMEM_BYTES),
        cost_estimate=pl.CostEstimate(
            flops=4 * rows * width * half, bytes_accessed=9 * 2**20, transcendentals=0
        ),
    )(slopes, weights)


def outer_kernel(x_early, x_late, dy_early, dy_late, slopes_early, slopes_late, hidden_early, hidden_late, out):
    def joined(early, late):
        return jnp.concatenate([early[...], late[...]], 0)

    def product(rows, values):
        return lax.dot_general(rows, values, OUTER, preferred_element_type=F32).astype(BF16)

    both = slopes_early.shape[1]
    out[:, :both] = product(joined(x_early, x_late), joined(slopes_early, slopes_late))
    out[:, both:] = product(joined(dy_early, dy_late), joined(hidden_early, hidden_late))


def outer_terms(rows_x, rows_dy, slopes, hidden):
    width, cut = rows_x[0].shape[1], 512
    columns = slopes[0].shape[1] + hidden[0].shape[1]
    return pl.pallas_call(
        outer_kernel,
        grid=(width // cut,),
        in_specs=[pl.BlockSpec((v.shape[0], cut), lambda k: (0, k)) for v in (*rows_x, *rows_dy)]
        + [pl.BlockSpec(v.shape, lambda k: (0, 0)) for v in (*slopes, *hidden)],
        out_specs=pl.BlockSpec((cut, columns), lambda k: (k, 0)),
        out_shape=jax.ShapeDtypeStruct((width, columns), BF16),
        compiler_params=pltpu.CompilerParams(vmem_limit_bytes=VMEM_BYTES),
        cost_estimate=pl.CostEstimate(flops=0, bytes_accessed=0, transcendentals=0),
    )(*rows_x, *rows_dy, *slopes, *hidden)


def local(layer_input, out_grad, routes, gates, w_gate, w_up, w_down):
    dev_count = lax.axis_size("expert")
    xs, zs = 4, dev_count // 4
    tok_rows, width = layer_input.shape[1:]
    experts = dev_count // 2
    capacity = 2 * tok_rows // experts
    me = lax.axis_index("expert")
    my_z, my_pair = me // xs, me % xs // 2

    tokens = layer_input[0]
    scaled = (gates[0][:, None] * out_grad[0].astype(F32)).astype(BF16)
    target = routes[0, :, 0]
    onehot = (target[:, None] == jnp.arange(experts, dtype=jnp.int32)[None, :]).astype(jnp.int32)
    before = jnp.cumsum(onehot, axis=0) - onehot
    rank = jnp.sum(before * onehot, axis=1)
    step = (target // 2 - my_z) % zs
    side = (target % 2) ^ my_pair
    home_column = (step * 2 + side) * capacity + rank
    other_column = lax.ppermute(home_column.astype(F32), "pipe", [(0, 1), (1, 0)])
    both = jnp.concatenate([tokens, scaled], axis=0)
    row_x = (step * 2 + side) * 2 * capacity + rank
    row_of = jnp.concatenate([row_x, row_x + capacity], axis=0)
    block_rows = 4 * capacity

    def block(s):
        rows = jnp.arange(block_rows, dtype=jnp.int32) + s * block_rows
        pick = (rows[:, None] == row_of[None, :]).astype(BF16)
        return jnp.dot(pick, both, preferred_element_type=F32).astype(BF16)

    blocks = [block(s) for s in range(zs)]
    here = {0: blocks[0]}
    shards = lax.optimization_barrier((w_gate, w_up, w_down, blocks[4]))[:3]
    weights = lax.all_gather(jnp.concatenate(shards, 0), "dp", axis=1, tiled=True)

    def round_of(sends, steps, *more):
        outs = []
        if steps:
            stacked = [here[s].reshape(2, 2, capacity, width) for s in steps]
            same = jnp.concatenate([v[0, part] for part in range(2) for v in stacked], 0)
            cross = jnp.concatenate([v[1, part] for part in range(2) for v in stacked], 0)
            outs = [same] + [
                moved(same, lambda i: to_mate(i, xs)),
                moved(cross, lambda i: to_other(i, xs)),
                moved(cross, lambda i: to_diagonal(i, xs)),
            ]
        spread = len(outs)
        for s in sends:
            outs.append(moved(blocks[s], lambda i, s=s: along_z(i, s, zs, xs)))
        names = [s for s in (0, 2, 6, 3, 5, 4) if s not in here]
        rest = [blocks[s] for s in names if s not in sends]
        done = lax.optimization_barrier(tuple(outs + rest) + more)
        if steps:
            parts.append(done[:spread])
        for s, v in zip(sends, done[spread:]):
            here[s] = v
        for s, v in zip([s for s in names if s not in sends], done[spread + len(sends):]):
            blocks[s] = v
        return done[len(done) - len(more):]

    rounds = [((1, 7), ()), ((2, 6), (1, 7)), ((3, 5), (2, 6, 0)), ((4,), (3, 5)), ((), (4,))]
    parts = []
    for sends, steps in rounds[:3]:
        round_of(sends, steps)

    def block_of(some):
        pieces = [g[origin] for origin in range(4) for g in some]
        return expert_block(pieces, weights, capacity)

    early = block_of(parts)
    early = round_of(*rounds[3], *early)
    early = tuple(early) + tuple(back_block(early[3], weights))
    early = round_of(*rounds[4], *early)

    def returned(back):
        return [
            moved(back[1], lambda i: to_mate(i, xs)),
            moved(back[2], lambda i: to_other(i, xs)),
            moved(back[3], lambda i: to_diagonal(i, xs)),
        ]

    def summed(back, came, steps):
        same = (back[0].astype(F32) + came[0].astype(F32)).astype(BF16)
        cross = (came[1].astype(F32) + came[2].astype(F32)).astype(BF16)
        for k, s in enumerate(steps):
            cut = slice(k * capacity, (k + 1) * capacity)
            homes[s] = jnp.concatenate([same[cut], cross[cut]], 0)

    def home(s):
        route = [
            (c * dev_count + i, (1 - c) * dev_count + along_z(i, -s, zs, xs))
            for c in range(2) for i in range(dev_count)
        ]
        return lax.ppermute(homes[s], ("pipe", "expert"), route)

    homes = {}
    late_steps = [s for r in rounds[3:] for s in r[1]]
    early_steps = [s for r in rounds[:3] for s in r[1]]
    late = block_of(parts[2:])
    hidden_late, *back_early = lax.optimization_barrier((late[2], *early[4:]))
    came = returned(back_early)
    rows_x, rows_dy, hidden, slopes = zip(early[:4], late)
    half = hidden[0].shape[1]
    terms = outer_terms(rows_x, rows_dy, slopes, (hidden[0], hidden_late))
    grads = lax.psum_scatter(terms, "dp", scatter_dimension=0, tiled=True)
    back_late = back_block(after(late[3], terms), weights)
    *came, b0, b1, b2, b3 = lax.optimization_barrier((*came, *back_late))
    summed(early[4:], came, early_steps)
    back_late = [b0, b1, b2, b3]
    came = returned(back_late)
    near = {s: home(s) for s in (2, 6)}
    came = list(lax.optimization_barrier((*came, near[2], near[6], *[homes[s] for s in (0, 1, 7)])))
    near = dict(zip((2, 6), came[3:5]))
    homes.update(zip((0, 1, 7), came[5:8]))
    summed(back_late, came[:3], late_steps)
    homes = {s: home(s) for s in (3, 5, 4, 1, 7, 0)} | near
    summed_rows = jnp.concatenate([homes[s] for s in range(zs)], 0)
    slots = jnp.arange(2 * zs * capacity, dtype=jnp.int32)
    combine = (slots[None, :] == other_column.astype(jnp.int32)[:, None]).astype(BF16)
    passed = jnp.dot(combine, summed_rows, preferred_element_type=F32).astype(BF16)
    passed, grads = lax.optimization_barrier((passed, grads))
    return (
        passed[None],
        grads[:, :half].astype(F32)[None],
        grads[:, half:2 * half].astype(F32)[None],
        grads[:, 2 * half:].astype(F32)[None],
    )


def solution(mesh):
    placed = (
        P("pipe", ("expert", "dp"), None),
        P("pipe", ("expert", "dp"), None),
        P("pipe", ("expert", "dp"), None),
        P("pipe", ("expert", "dp")),
        P("pipe", "dp", "expert"),
        P("pipe", "dp", "expert"),
        P("pipe", "dp", "expert"),
    )
    return jax.shard_map(
        local,
        mesh=mesh,
        in_specs=placed,
        out_specs=(
            P("pipe", ("expert", "dp"), None),
            P("pipe", "dp", "expert"),
            P("pipe", "dp", "expert"),
            P("pipe", "dp", "expert"),
        ),
        check_vma=False,
    )
```

profile of v0, /device:TPU:1, one launch (start us, length us, event | category | flops | bytes accessed | tf_op | source)
XLA Modules:
  0.0 279.7 jit_solution(4212201395272386663)
XLA Ops:
  15.5 2.5 collective-permute-start.1
  18.5 4.0 %collective-permute-start.2 = (bf16[64,4096]{1,0:T(8,128)(2,1)S(1)}, bf16[64,4096]{1,0:T(8,128)(2,1)S(1)}, u32[]{:S(2)}, u32[]{:S(2)}) collective-permute-start(bf16[64,4096]{1,0:T(8,128)(2,1)S(1)} %convolution_convert_fusion.7), channel_id=1, source_target_pairs={{0,112},{4,116},{8,120},{12,124},{16,0},{20,4},{24,8},{28,12},{32,... | collective-permute-start | bytes 1572872 | tf_op jit(solution)/shard_map/ppermute | solution.py:35
  24.7 8.9 %collective-permute-done.1 = bf16[64,4096]{1,0:T(8,128)(2,1)S(1)} collective-permute-done((bf16[64,4096]{1,0:T(8,128)(2,1)S(1)}, bf16[64,4096]{1,0:T(8,128)(2,1)S(1)}, u32[]{:S(2)}, u32[]{:S(2)}) %collective-permute-start.1) | collective-permute-done | bytes 524320 | tf_op jit(solution)/shard_map/ppermute | solution.py:35
  33.7 2.8 %collective-permute-start.5 = (bf16[64,4096]{1,0:T(8,128)(2,1)S(1)}, bf16[64,4096]{1,0:T(8,128)(2,1)S(1)}, u32[]{:S(2)}, u32[]{:S(2)}) collective-permute-start(bf16[64,4096]{1,0:T(8,128)(2,1)S(1)} %pad_maximum_fusion.3), channel_id=1, source_target_pairs={{0,8},{4,12},{8,0},{12,4},{16,24},{20,28},{24,16},{28,20},{32,40},... | collective-permute-start | bytes 1572872 | tf_op jit(solution)/shard_map/ppermute | solution.py:35
  41.7 17.2 %collective-permute-done.3.refs_2_ = bf16[64,4096]{1,0:T(8,128)(2,1)S(1)} collective-permute-done((bf16[64,4096]{1,0:T(8,128)(2,1)S(1)}, bf16[64,4096]{1,0:T(8,128)(2,1)S(1)}, u32[]{:S(2)}, u32[]{:S(2)}) %collective-permute-start.3) | collective-permute-done | bytes 524320 | tf_op jit(solution)/shard_map/ppermute | solution.py:35
  62.2 2.7 collective-permute-start.9
  64.9 6.7 %collective-permute-start.11 = (bf16[64,4096]{1,0:T(8,128)(2,1)S(1)}, bf16[64,4096]{1,0:T(8,128)(2,1)S(1)}, u32[]{:S(2)}, u32[]{:S(2)}) collective-permute-start(bf16[64,4096]{1,0:T(8,128)(2,1)S(1)} %convolution_convert_fusion.4), channel_id=1, source_target_pairs={{0,48},{4,52},{8,56},{12,60},{16,64},{20,68},{24,72},{28,76},{32,8... | collective-permute-start | bytes 1572872 | tf_op jit(solution)/shard_map/ppermute | solution.py:35
  72.1 26.3 %collective-permute-done.11 = bf16[64,4096]{1,0:T(8,128)(2,1)S(1)} collective-permute-done((bf16[64,4096]{1,0:T(8,128)(2,1)S(1)}, bf16[64,4096]{1,0:T(8,128)(2,1)S(1)}, u32[]{:S(2)}, u32[]{:S(2)}) %collective-permute-start.11) | collective-permute-done | bytes 524320 | tf_op jit(solution)/shard_map/ppermute | solution.py:35
  98.5 5.8 %collective-permute-done.12 = bf16[64,4096]{1,0:T(8,128)(2,1)S(1)} collective-permute-done((bf16[64,4096]{1,0:T(8,128)(2,1)S(1)}, bf16[64,4096]{1,0:T(8,128)(2,1)S(1)}, u32[]{:S(2)}, u32[]{:S(2)}) %collective-permute-start.12) | collective-permute-done | bytes 524320 | tf_op jit(solution)/shard_map/ppermute | solution.py:35
  110.3 5.4 %collective-permute-start.16 = (bf16[64,4096]{1,0:T(8,128)(2,1)}, bf16[64,4096]{1,0:T(8,128)(2,1)S(1)}, u32[]{:S(2)}, u32[]{:S(2)}) collective-permute-start(bf16[64,4096]{1,0:T(8,128)(2,1)} %convolution_convert_fusion.2), channel_id=1, source_target_pairs={{0,64},{4,68},{8,72},{12,76},{16,80},{20,84},{24,88},{28,92},{32,9... | collective-permute-start | bytes 1572872 | tf_op jit(solution)/shard_map/ppermute | solution.py:35
  115.7 9.6 %shard_map.102 = (bf16[320,4096]{1,0:T(8,128)(2,1)}, bf16[320,4096]{1,0:T(8,128)(2,1)}, bf16[320,384]{1,0:T(8,128)(2,1)}, bf16[320,768]{1,0:T(8,128)(2,1)}) custom-call(bf16[64,4096]{1,0:T(8,128)(2,1)} %copy-done, bf16[96,4096]{1,0:T(8,128)(2,1)} %copy-done.2, bf16[64,4096]{1,0:T(8,128)(2,1)} %copy-done.13, bf16[96,4096]{1,0:T(8,128)(2,1)} %copy-done.6, ...), custom_call_target="tpu_custom_call" | custom-call | flops 3019898880 | bytes 20971520 | tf_op jit(solution)/shard_map/pallas_call | solution.py:105
  127.6 10.0 %collective-permute-done.16 = bf16[64,4096]{1,0:T(8,128)(2,1)S(1)} collective-permute-done((bf16[64,4096]{1,0:T(8,128)(2,1)}, bf16[64,4096]{1,0:T(8,128)(2,1)S(1)}, u32[]{:S(2)}, u32[]{:S(2)}) %collective-permute-start.16) | collective-permute-done | bytes 524320 | tf_op jit(solution)/shard_map/ppermute | solution.py:35
  137.9 3.0 %collective-permute-start.19 = (bf16[32,4096]{1,0:T(8,128)(2,1)S(1)}, bf16[32,4096]{1,0:T(8,128)(2,1)S(1)}, u32[]{:S(2)}, u32[]{:S(2)}) collective-permute-start(bf16[32,4096]{1,0:T(8,128)(2,1)S(1)} %pad_maximum_fusion.7), channel_id=1, source_target_pairs={{0,8},{4,12},{8,0},{12,4},{16,24},{20,28},{24,16},{28,20},{32,40},... | collective-permute-start | bytes 786440 | tf_op jit(solution)/shard_map/ppermute | solution.py:35
  141.7 6.7 %shard_map.103 = (bf16[80,4096]{1,0:T(8,128)(2,1)}, bf16[80,4096]{1,0:T(8,128)(2,1)}, bf16[80,4096]{1,0:T(8,128)(2,1)}, bf16[80,4096]{1,0:T(8,128)(2,1)}) custom-call(bf16[320,768]{1,0:T(8,128)(2,1)} %get-tuple-element.149.slopes.slopes_early, bf16[3,4096,384]{2,1,0:T(8,128)(2,1)} %all-gather.2.cloned.1.call-done.refs_8_.weights), custom_call_target="tpu_custom_call" | custom-call | flops 2013265920 | bytes 9437184 | tf_op jit(solution)/shard_map/pallas_call | solution.py:143
  149.8 4.5 %collective-permute-done.18.refs_5_ = bf16[32,4096]{1,0:T(8,128)(2,1)S(1)} collective-permute-done((bf16[32,4096]{1,0:T(8,128)(2,1)S(1)}, bf16[32,4096]{1,0:T(8,128)(2,1)S(1)}, u32[]{:S(2)}, u32[]{:S(2)}) %collective-permute-start.18) | collective-permute-done | bytes 262176 | tf_op jit(solution)/shard_map/ppermute | solution.py:35
  155.0 7.3 %shard_map.104 = (bf16[192,4096]{1,0:T(8,128)(2,1)}, bf16[192,4096]{1,0:T(8,128)(2,1)}, bf16[192,384]{1,0:T(8,128)(2,1)}, bf16[192,768]{1,0:T(8,128)(2,1)}) custom-call(bf16[64,4096]{1,0:T(8,128)(2,1)} %copy-done.1, bf16[32,4096]{1,0:T(8,128)(2,1)} %copy-done.3, bf16[64,4096]{1,0:T(8,128)(2,1)} %copy-done.14, bf16[32,4096]{1,0:T(8,128)(2,1)} %copy-done.17, ...), custom_call_target="tpu_custom_call" | custom-call | flops 1811939328 | bytes 20971520 | tf_op jit(solution)/shard_map/pallas_call | solution.py:105
  162.3 12.3 %shard_map.105 = bf16[4096,1152]{1,0:T(8,128)(2,1)} custom-call(bf16[320,4096]{1,0:T(8,128)(2,1)} %get-tuple-element.145.x_early, bf16[192,4096]{1,0:T(8,128)(2,1)} %get-tuple-element.146.x_late, bf16[320,4096]{1,0:T(8,128)(2,1)} %get-tuple-element.147.dy_early, bf16[192,4096]{1,0:T(8,128)(2,1)} %get-tuple-element.148.dy_late, ...), custom_call_target="tpu_custom_call" | custom-call | tf_op jit(solution)/shard_map/pallas_call | solution.py:174
  178.9 3.0 %collective-permute-start = (f32[128]{0:T(128)S(1)}, f32[128]{0:T(128)S(1)}, u32[]{:S(2)}, u32[]{:S(2)}) collective-permute-start(f32[128]{0:T(128)S(1)} %get-tuple-element.174), channel_id=1, source_target_pairs={{0,128},{128,0},{1,129},{129,1},{2,130},{130,2},{3,131},{131,3},{4... | collective-permute-start | bytes 1544 | tf_op jit(solution)/shard_map/ppermute | solution.py:204
  182.7 6.1 %shard_map.106 = (bf16[48,4096]{1,0:T(8,128)(2,1)}, bf16[48,4096]{1,0:T(8,128)(2,1)}, bf16[48,4096]{1,0:T(8,128)(2,1)}, bf16[48,4096]{1,0:T(8,128)(2,1)}) custom-call(bf16[192,768]{1,0:T(8,128)(2,1)} %get-tuple-element.152.slopes_late.slopes, bf16[3,4096,384]{2,1,0:T(8,128)(2,1)} %all-gather.2.cloned.1.call-done.refs_8_.weights), custom_call_target="tpu_custom_call" | custom-call | flops 1207959552 | bytes 9437184 | tf_op jit(solution)/shard_map/pallas_call | solution.py:143
  189.9 2.3 collective-permute-done.21
  192.2 12.2 %collective-permute-done.22 = bf16[80,4096]{1,0:T(8,128)(2,1)S(1)} collective-permute-done((bf16[80,4096]{1,0:T(8,128)(2,1)S(1)}, bf16[80,4096]{1,0:T(8,128)(2,1)S(1)}, u32[]{:S(2)}, u32[]{:S(2)}) %collective-permute-start.22) | collective-permute-done | bytes 655392 | tf_op jit(solution)/shard_map/ppermute | solution.py:35
  208.2 2.7 collective-permute-start.27
  211.0 8.3 %collective-permute-done.26 = bf16[32,4096]{1,0:T(8,128)(2,1)S(1)} collective-permute-done((bf16[32,4096]{1,0:T(8,128)(2,1)S(1)}, bf16[32,4096]{1,0:T(8,128)(2,1)S(1)}, u32[]{:S(2)}, u32[]{:S(2)}) %collective-permute-start.26) | collective-permute-done | bytes 262176 | tf_op jit(solution)/shard_map/ppermute | solution.py:278
  219.3 4.3 %collective-permute-done.27 = bf16[32,4096]{1,0:T(8,128)(2,1)S(1)} collective-permute-done((bf16[32,4096]{1,0:T(8,128)(2,1)S(1)}, bf16[32,4096]{1,0:T(8,128)(2,1)S(1)}, u32[]{:S(2)}, u32[]{:S(2)}) %collective-permute-start.27) | collective-permute-done | bytes 262176 | tf_op jit(solution)/shard_map/ppermute | solution.py:278
  223.6 3.4 %collective-permute-start.28 = (bf16[32,4096]{1,0:T(8,128)(2,1)S(1)}, bf16[32,4096]{1,0:T(8,128)(2,1)S(1)}, u32[]{:S(2)}, u32[]{:S(2)}) collective-permute-start(bf16[32,4096]{1,0:T(8,128)(2,1)S(1)} %pad_maximum_fusion.10), channel_id=1, source_target_pairs={{0,128},{4,132},{8,136},{12,140},{16,144},{20,148},{24,152},{28,15... | collective-permute-start | bytes 786440 | tf_op jit(solution)/shard_map/ppermute | solution.py:278
  229.0 3.7 %collective-permute-start.30 = (bf16[32,4096]{1,0:T(8,128)(2,1)S(1)}, bf16[32,4096]{1,0:T(8,128)(2,1)S(1)}, u32[]{:S(2)}, u32[]{:S(2)}) collective-permute-start(bf16[32,4096]{1,0:T(8,128)(2,1)S(1)} %pad_maximum_fusion.13), channel_id=1, source_target_pairs={{0,208},{4,212},{8,216},{12,220},{16,224},{20,228},{24,232},{28,23... | collective-permute-start | bytes 786440 | tf_op jit(solution)/shard_map/ppermute | solution.py:278
  234.3 3.3 %collective-permute-start.32 = (bf16[32,4096]{1,0:T(8,128)(2,1)S(1)}, bf16[32,4096]{1,0:T(8,128)(2,1)S(1)}, u32[]{:S(2)}, u32[]{:S(2)}) collective-permute-start(bf16[32,4096]{1,0:T(8,128)(2,1)S(1)} %pad_maximum_fusion.15), channel_id=1, source_target_pairs={{0,176},{4,180},{8,184},{12,188},{16,192},{20,196},{24,200},{28,20... | collective-permute-start | bytes 786440 | tf_op jit(solution)/shard_map/ppermute | solution.py:278
  237.6 2.5 collective-permute-done.29
  240.2 6.3 %collective-permute-done.30 = bf16[32,4096]{1,0:T(8,128)(2,1)S(1)} collective-permute-done((bf16[32,4096]{1,0:T(8,128)(2,1)S(1)}, bf16[32,4096]{1,0:T(8,128)(2,1)S(1)}, u32[]{:S(2)}, u32[]{:S(2)}) %collective-permute-start.30) | collective-permute-done | bytes 262176 | tf_op jit(solution)/shard_map/ppermute | solution.py:278
  246.5 5.2 %collective-permute-done.31 = bf16[32,4096]{1,0:T(8,128)(2,1)S(1)} collective-permute-done((bf16[32,4096]{1,0:T(8,128)(2,1)S(1)}, bf16[32,4096]{1,0:T(8,128)(2,1)S(1)}, u32[]{:S(2)}, u32[]{:S(2)}) %collective-permute-start.31) | collective-permute-done | bytes 262176 | tf_op jit(solution)/shard_map/ppermute | solution.py:278
  251.8 15.6 %collective-permute-done.32 = bf16[32,4096]{1,0:T(8,128)(2,1)S(1)} collective-permute-done((bf16[32,4096]{1,0:T(8,128)(2,1)S(1)}, bf16[32,4096]{1,0:T(8,128)(2,1)S(1)}, u32[]{:S(2)}, u32[]{:S(2)}) %collective-permute-start.32) | collective-permute-done | bytes 262176 | tf_op jit(solution)/shard_map/ppermute | solution.py:278
  268.9 3.9 %bitcast_convert_fusion = (f32[1,1024,384]{2,1,0:T(8,128)}, f32[1,1024,384]{2,1,0:T(8,128)}, f32[1,1024,384]{2,1,0:T(8,128)}) fusion(bf16[1024,1152]{1,0:T(8,128)(2,1)} %reduce-scatter.2.cloned.1.call-done), kind=kLoop, calls=%fused_computation.15 | loop fusion | flops 1179648 | bytes 7077888 | tf_op jit(solution)/shard_map/broadcast_in_dim | solution.py:310
  (163 shorter events, 46.5 us)
Async XLA Ops:
  7.2 108.5 %all-gather.2.cloned.1.call-start = ((), (), s32[]{:S(2)}) async-start(), calls=%async_computation.1 | async-start | bytes 11796480 | tf_op jit(solution)/shard_map/all_gather | solution.py:218
  14.9 254.1 %reduce-scatter.2.cloned.1.call-start = ((), (), s32[]{:S(2)}) async-start(), calls=%async_computation.2 | async-start | bytes 11796480 | tf_op jit(solution)/shard_map/reduce_scatter | solution.py:289
  15.5 18.1 %collective-permute-start.1 = (bf16[64,4096]{1,0:T(8,128)(2,1)S(1)}, bf16[64,4096]{1,0:T(8,128)(2,1)S(1)}, u32[]{:S(2)}, u32[]{:S(2)}) collective-permute-start(bf16[64,4096]{1,0:T(8,128)(2,1)S(1)} %convolution_convert_fusion.8), channel_id=1, source_target_pairs={{0,16},{4,20},{8,24},{12,28},{16,32},{20,36},{24,40},{28,44},{32,4... | collective-permute-start | bytes 1572872 | tf_op jit(solution)/shard_map/ppermute | solution.py:35
  18.5 15.1 %collective-permute-start.2 = (bf16[64,4096]{1,0:T(8,128)(2,1)S(1)}, bf16[64,4096]{1,0:T(8,128)(2,1)S(1)}, u32[]{:S(2)}, u32[]{:S(2)}) collective-permute-start(bf16[64,4096]{1,0:T(8,128)(2,1)S(1)} %convolution_convert_fusion.7), channel_id=1, source_target_pairs={{0,112},{4,116},{8,120},{12,124},{16,0},{20,4},{24,8},{28,12},{32,... | collective-permute-start | bytes 1572872 | tf_op jit(solution)/shard_map/ppermute | solution.py:35
  33.7 25.2 %collective-permute-start.5 = (bf16[64,4096]{1,0:T(8,128)(2,1)S(1)}, bf16[64,4096]{1,0:T(8,128)(2,1)S(1)}, u32[]{:S(2)}, u32[]{:S(2)}) collective-permute-start(bf16[64,4096]{1,0:T(8,128)(2,1)S(1)} %pad_maximum_fusion.3), channel_id=1, source_target_pairs={{0,8},{4,12},{8,0},{12,4},{16,24},{20,28},{24,16},{28,20},{32,40},... | collective-permute-start | bytes 1572872 | tf_op jit(solution)/shard_map/ppermute | solution.py:35
  36.6 23.9 %collective-permute-start.4 = (bf16[64,4096]{1,0:T(8,128)(2,1)S(1)}, bf16[64,4096]{1,0:T(8,128)(2,1)S(1)}, u32[]{:S(2)}, u32[]{:S(2)}) collective-permute-start(bf16[64,4096]{1,0:T(8,128)(2,1)S(1)} %pad_maximum_fusion.3), channel_id=1, source_target_pairs={{0,12},{4,8},{8,4},{12,0},{16,28},{20,24},{24,20},{28,16},{32,44},... | collective-permute-start | bytes 1572872 | tf_op jit(solution)/shard_map/ppermute | solution.py:35
  37.5 21.5 %collective-permute-start.3 = (bf16[64,4096]{1,0:T(8,128)(2,1)S(1)}, bf16[64,4096]{1,0:T(8,128)(2,1)S(1)}, u32[]{:S(2)}, u32[]{:S(2)}) collective-permute-start(bf16[64,4096]{1,0:T(8,128)(2,1)S(1)} %pad_maximum_fusion.2.refs_0_), channel_id=1, source_target_pairs={{0,4},{4,0},{8,12},{12,8},{16,20},{20,16},{24,28},{28,24},{32,36},... | collective-permute-start | bytes 1572872 | tf_op jit(solution)/shard_map/ppermute | solution.py:35
  37.6 22.9 %collective-permute-start.6 = (bf16[64,4096]{1,0:T(8,128)(2,1)S(1)}, bf16[64,4096]{1,0:T(8,128)(2,1)S(1)}, u32[]{:S(2)}, u32[]{:S(2)}) collective-permute-start(bf16[64,4096]{1,0:T(8,128)(2,1)S(1)} %convolution_convert_fusion.6), channel_id=1, source_target_pairs={{0,32},{4,36},{8,40},{12,44},{16,48},{20,52},{24,56},{28,60},{32,6... | collective-permute-start | bytes 1572872 | tf_op jit(solution)/shard_map/ppermute | solution.py:35
  39.8 20.7 %collective-permute-start.7 = (bf16[64,4096]{1,0:T(8,128)(2,1)S(1)}, bf16[64,4096]{1,0:T(8,128)(2,1)S(1)}, u32[]{:S(2)}, u32[]{:S(2)}) collective-permute-start(bf16[64,4096]{1,0:T(8,128)(2,1)S(1)} %convolution_convert_fusion.5), channel_id=1, source_target_pairs={{0,96},{4,100},{8,104},{12,108},{16,112},{20,116},{24,120},{28,124... | collective-permute-start | bytes 1572872 | tf_op jit(solution)/shard_map/ppermute | solution.py:35
  61.3 42.9 %collective-permute-start.10 = (bf16[96,4096]{1,0:T(8,128)(2,1)S(1)}, bf16[96,4096]{1,0:T(8,128)(2,1)S(1)}, u32[]{:S(2)}, u32[]{:S(2)}) collective-permute-start(bf16[96,4096]{1,0:T(8,128)(2,1)S(1)} %get-tuple-element.203), channel_id=1, source_target_pairs={{0,8},{4,12},{8,0},{12,4},{16,24},{20,28},{24,16},{28,20},{32,40},... | collective-permute-start | bytes 2359304 | tf_op jit(solution)/shard_map/ppermute | solution.py:35
  62.2 42.0 %collective-permute-start.9 = (bf16[96,4096]{1,0:T(8,128)(2,1)S(1)}, bf16[96,4096]{1,0:T(8,128)(2,1)S(1)}, u32[]{:S(2)}, u32[]{:S(2)}) collective-permute-start(bf16[96,4096]{1,0:T(8,128)(2,1)S(1)} %get-tuple-element.203), channel_id=1, source_target_pairs={{0,12},{4,8},{8,4},{12,0},{16,28},{20,24},{24,20},{28,16},{32,44},... | collective-permute-start | bytes 2359304 | tf_op jit(solution)/shard_map/ppermute | solution.py:35
  64.9 39.4 %collective-permute-start.8 = (bf16[96,4096]{1,0:T(8,128)(2,1)S(1)}, bf16[96,4096]{1,0:T(8,128)(2,1)S(1)}, u32[]{:S(2)}, u32[]{:S(2)}) collective-permute-start(bf16[96,4096]{1,0:T(8,128)(2,1)S(1)} %get-tuple-element.105.refs_1_), channel_id=1, source_target_pairs={{0,4},{4,0},{8,12},{12,8},{16,20},{20,16},{24,28},{28,24},{32,36},... | collective-permute-start | bytes 2359304 | tf_op jit(solution)/shard_map/ppermute | solution.py:35
  64.9 33.6 %collective-permute-start.11 = (bf16[64,4096]{1,0:T(8,128)(2,1)S(1)}, bf16[64,4096]{1,0:T(8,128)(2,1)S(1)}, u32[]{:S(2)}, u32[]{:S(2)}) collective-permute-start(bf16[64,4096]{1,0:T(8,128)(2,1)S(1)} %convolution_convert_fusion.4), channel_id=1, source_target_pairs={{0,48},{4,52},{8,56},{12,60},{16,64},{20,68},{24,72},{28,76},{32,8... | collective-permute-start | bytes 1572872 | tf_op jit(solution)/shard_map/ppermute | solution.py:35
  71.6 32.6 %collective-permute-start.12 = (bf16[64,4096]{1,0:T(8,128)(2,1)S(1)}, bf16[64,4096]{1,0:T(8,128)(2,1)S(1)}, u32[]{:S(2)}, u32[]{:S(2)}) collective-permute-start(bf16[64,4096]{1,0:T(8,128)(2,1)S(1)} %convolution_convert_fusion.3), channel_id=1, source_target_pairs={{0,80},{4,84},{8,88},{12,92},{16,96},{20,100},{24,104},{28,108},{3... | collective-permute-start | bytes 1572872 | tf_op jit(solution)/shard_map/ppermute | solution.py:35
  105.4 19.9 %collective-permute-start.13 = (bf16[64,4096]{1,0:T(8,128)(2,1)S(1)}, bf16[64,4096]{1,0:T(8,128)(2,1)S(1)}, u32[]{:S(2)}, u32[]{:S(2)}) collective-permute-start(bf16[64,4096]{1,0:T(8,128)(2,1)S(1)} %pad_maximum_fusion.4.refs_0_), channel_id=1, source_target_pairs={{0,4},{4,0},{8,12},{12,8},{16,20},{20,16},{24,28},{28,24},{32,36},... | collective-permute-start | bytes 1572872 | tf_op jit(solution)/shard_map/ppermute | solution.py:35
  107.7 19.9 %collective-permute-start.15 = (bf16[64,4096]{1,0:T(8,128)(2,1)}, bf16[64,4096]{1,0:T(8,128)(2,1)}, u32[]{:S(2)}, u32[]{:S(2)}) collective-permute-start(bf16[64,4096]{1,0:T(8,128)(2,1)} %pad_maximum_fusion.5), channel_id=1, source_target_pairs={{0,8},{4,12},{8,0},{12,4},{16,24},{20,28},{24,16},{28,20},{32,40},... | collective-permute-start | bytes 1572872 | tf_op jit(solution)/shard_map/ppermute | solution.py:35
  109.4 18.2 %collective-permute-start.14 = (bf16[64,4096]{1,0:T(8,128)(2,1)}, bf16[64,4096]{1,0:T(8,128)(2,1)S(1)}, u32[]{:S(2)}, u32[]{:S(2)}) collective-permute-start(bf16[64,4096]{1,0:T(8,128)(2,1)} %pad_maximum_fusion.5), channel_id=1, source_target_pairs={{0,12},{4,8},{8,4},{12,0},{16,28},{20,24},{24,20},{28,16},{32,44},... | collective-permute-start | bytes 1572872 | tf_op jit(solution)/shard_map/ppermute | solution.py:35
  110.3 27.3 %collective-permute-start.16 = (bf16[64,4096]{1,0:T(8,128)(2,1)}, bf16[64,4096]{1,0:T(8,128)(2,1)S(1)}, u32[]{:S(2)}, u32[]{:S(2)}) collective-permute-start(bf16[64,4096]{1,0:T(8,128)(2,1)} %convolution_convert_fusion.2), channel_id=1, source_target_pairs={{0,64},{4,68},{8,72},{12,76},{16,80},{20,84},{24,88},{28,92},{32,9... | collective-permute-start | bytes 1572872 | tf_op jit(solution)/shard_map/ppermute | solution.py:35
  137.9 11.9 %collective-permute-start.19 = (bf16[32,4096]{1,0:T(8,128)(2,1)S(1)}, bf16[32,4096]{1,0:T(8,128)(2,1)S(1)}, u32[]{:S(2)}, u32[]{:S(2)}) collective-permute-start(bf16[32,4096]{1,0:T(8,128)(2,1)S(1)} %pad_maximum_fusion.7), channel_id=1, source_target_pairs={{0,8},{4,12},{8,0},{12,4},{16,24},{20,28},{24,16},{28,20},{32,40},... | collective-permute-start | bytes 786440 | tf_op jit(solution)/shard_map/ppermute | solution.py:35
  140.9 13.4 %collective-permute-start.18 = (bf16[32,4096]{1,0:T(8,128)(2,1)S(1)}, bf16[32,4096]{1,0:T(8,128)(2,1)S(1)}, u32[]{:S(2)}, u32[]{:S(2)}) collective-permute-start(bf16[32,4096]{1,0:T(8,128)(2,1)S(1)} %pad_maximum_fusion.7), channel_id=1, source_target_pairs={{0,12},{4,8},{8,4},{12,0},{16,28},{20,24},{24,20},{28,16},{32,44},... | collective-permute-start | bytes 786440 | tf_op jit(solution)/shard_map/ppermute | solution.py:35
  175.7 14.2 %collective-permute-start.20 = (bf16[80,4096]{1,0:T(8,128)(2,1)S(1)}, bf16[80,4096]{1,0:T(8,128)(2,1)S(1)}, u32[]{:S(2)}, u32[]{:S(2)}) collective-permute-start(bf16[80,4096]{1,0:T(8,128)(2,1)S(1)} %copy-done.24), channel_id=1, source_target_pairs={{0,4},{4,0},{8,12},{12,8},{16,20},{20,16},{24,28},{28,24},{32,36},... | collective-permute-start | bytes 1966088 | tf_op jit(solution)/shard_map/ppermute | solution.py:35
  175.9 16.3 %collective-permute-start.21 = (bf16[80,4096]{1,0:T(8,128)(2,1)S(1)}, bf16[80,4096]{1,0:T(8,128)(2,1)S(1)}, u32[]{:S(2)}, u32[]{:S(2)}) collective-permute-start(bf16[80,4096]{1,0:T(8,128)(2,1)S(1)} %copy-done.23), channel_id=1, source_target_pairs={{0,12},{4,8},{8,4},{12,0},{16,28},{20,24},{24,20},{28,16},{32,44},... | collective-permute-start | bytes 1966088 | tf_op jit(solution)/shard_map/ppermute | solution.py:35
  176.7 27.7 %collective-permute-start.22 = (bf16[80,4096]{1,0:T(8,128)(2,1)S(1)}, bf16[80,4096]{1,0:T(8,128)(2,1)S(1)}, u32[]{:S(2)}, u32[]{:S(2)}) collective-permute-start(bf16[80,4096]{1,0:T(8,128)(2,1)S(1)} %copy-done.22), channel_id=1, source_target_pairs={{0,8},{4,12},{8,0},{12,4},{16,24},{20,28},{24,16},{28,20},{32,40},... | collective-permute-start | bytes 1966088 | tf_op jit(solution)/shard_map/ppermute | solution.py:35
  204.4 19.2 %collective-permute-start.23 = (bf16[48,4096]{1,0:T(8,128)(2,1)}, bf16[48,4096]{1,0:T(8,128)(2,1)S(1)}, u32[]{:S(2)}, u32[]{:S(2)}) collective-permute-start(bf16[48,4096]{1,0:T(8,128)(2,1)} %get-tuple-element.157), channel_id=1, source_target_pairs={{0,4},{4,0},{8,12},{12,8},{16,20},{20,16},{24,28},{28,24},{32,36},... | collective-permute-start | bytes 1179656 | tf_op jit(solution)/shard_map/ppermute | solution.py:35
  204.4 19.2 %collective-permute-start.24 = (bf16[48,4096]{1,0:T(8,128)(2,1)}, bf16[48,4096]{1,0:T(8,128)(2,1)S(1)}, u32[]{:S(2)}, u32[]{:S(2)}) collective-permute-start(bf16[48,4096]{1,0:T(8,128)(2,1)} %get-tuple-element.158), channel_id=1, source_target_pairs={{0,12},{4,8},{8,4},{12,0},{16,28},{20,24},{24,20},{28,16},{32,44},... | collective-permute-start | bytes 1179656 | tf_op jit(solution)/shard_map/ppermute | solution.py:35
  206.2 17.4 %collective-permute-start.25 = (bf16[48,4096]{1,0:T(8,128)(2,1)}, bf16[48,4096]{1,0:T(8,128)(2,1)S(1)}, u32[]{:S(2)}, u32[]{:S(2)}) collective-permute-start(bf16[48,4096]{1,0:T(8,128)(2,1)} %get-tuple-element.159), channel_id=1, source_target_pairs={{0,8},{4,12},{8,0},{12,4},{16,24},{20,28},{24,16},{28,20},{32,40},... | collective-permute-start | bytes 1179656 | tf_op jit(solution)/shard_map/ppermute | solution.py:35
  208.2 15.4 %collective-permute-start.27 = (bf16[32,4096]{1,0:T(8,128)(2,1)S(1)}, bf16[32,4096]{1,0:T(8,128)(2,1)S(1)}, u32[]{:S(2)}, u32[]{:S(2)}) collective-permute-start(bf16[32,4096]{1,0:T(8,128)(2,1)S(1)} %pad_maximum_fusion.9), channel_id=1, source_target_pairs={{0,160},{4,164},{8,168},{12,172},{16,176},{20,180},{24,184},{28,18... | collective-permute-start | bytes 786440 | tf_op jit(solution)/shard_map/ppermute | solution.py:278
  227.0 13.2 %collective-permute-start.29 = (bf16[32,4096]{1,0:T(8,128)(2,1)S(1)}, bf16[32,4096]{1,0:T(8,128)(2,1)S(1)}, u32[]{:S(2)}, u32[]{:S(2)}) collective-permute-start(bf16[32,4096]{1,0:T(8,128)(2,1)S(1)} %pad_maximum_fusion.11), channel_id=1, source_target_pairs={{0,240},{4,244},{8,248},{12,252},{16,128},{20,132},{24,136},{28,14... | collective-permute-start | bytes 786440 | tf_op jit(solution)/shard_map/ppermute | solution.py:278
  227.2 40.3 %collective-permute-start.33 = (bf16[32,4096]{1,0:T(8,128)(2,1)S(1)}, bf16[32,4096]{1,0:T(8,128)(2,1)S(1)}, u32[]{:S(2)}, u32[]{:S(2)}) collective-permute-start(bf16[32,4096]{1,0:T(8,128)(2,1)S(1)} %pad_maximum_fusion.12), channel_id=1, source_target_pairs={{0,144},{4,148},{8,152},{12,156},{16,160},{20,164},{24,168},{28,17... | collective-permute-start | bytes 786440 | tf_op jit(solution)/shard_map/ppermute | solution.py:278
  229.0 17.5 %collective-permute-start.30 = (bf16[32,4096]{1,0:T(8,128)(2,1)S(1)}, bf16[32,4096]{1,0:T(8,128)(2,1)S(1)}, u32[]{:S(2)}, u32[]{:S(2)}) collective-permute-start(bf16[32,4096]{1,0:T(8,128)(2,1)S(1)} %pad_maximum_fusion.13), channel_id=1, source_target_pairs={{0,208},{4,212},{8,216},{12,220},{16,224},{20,228},{24,232},{28,23... | collective-permute-start | bytes 786440 | tf_op jit(solution)/shard_map/ppermute | solution.py:278
  232.8 19.0 %collective-permute-start.31 = (bf16[32,4096]{1,0:T(8,128)(2,1)S(1)}, bf16[32,4096]{1,0:T(8,128)(2,1)S(1)}, u32[]{:S(2)}, u32[]{:S(2)}) collective-permute-start(bf16[32,4096]{1,0:T(8,128)(2,1)S(1)} %pad_maximum_fusion.14), channel_id=1, source_target_pairs={{0,192},{4,196},{8,200},{12,204},{16,208},{20,212},{24,216},{28,22... | collective-permute-start | bytes 786440 | tf_op jit(solution)/shard_map/ppermute | solution.py:278
  234.3 33.0 %collective-permute-start.32 = (bf16[32,4096]{1,0:T(8,128)(2,1)S(1)}, bf16[32,4096]{1,0:T(8,128)(2,1)S(1)}, u32[]{:S(2)}, u32[]{:S(2)}) collective-permute-start(bf16[32,4096]{1,0:T(8,128)(2,1)S(1)} %pad_maximum_fusion.15), channel_id=1, source_target_pairs={{0,176},{4,180},{8,184},{12,188},{16,192},{20,196},{24,200},{28,20... | collective-permute-start | bytes 786440 | tf_op jit(solution)/shard_map/ppermute | solution.py:278
  (29 other events, 315.1 us)
Sparse Core Ops, SparseCore 0:
  15.0 98.3 all-gather.1
  174.7 92.5 reduce-scatter.1
where the time goes:
time: 280 us
  waiting for transfers between devices  137 us (49%)
  starting transfers between devices  64.1 us (23%)
  Pallas kernels  41.9 us (15%)
  between operations  14.7 us (5%)
  other arithmetic  11.3 us (4%)
  matrix products  6.37 us (2%)
  local copies, waits for them, and re-layouts  4.59 us (2%)
    ppermute x25, waiting for transfers between devices, moved(): lax.ppermute(block, 'expert', [(i, place(i)) for i in range(lax.axis_size...  93.5 us
    ppermute x25, starting transfers between devices, moved(): lax.ppermute(block, 'expert', [(i, place(i)) for i in range(lax.axis_size...  44.7 us
    ppermute x8, waiting for transfers between devices, home(): return lax.ppermute(homes[s], ('pipe', 'expert'), route)  42.3 us
    pallas_call x2, Pallas kernels, expert_block(): pl.pallas_call(functools.partial(expert_kernel, counts, capacity), in_spe...  16.9 us
    ppermute x8, starting transfers between devices, home(): return lax.ppermute(homes[s], ('pipe', 'expert'), route)  16.4 us
    pallas_call x2, Pallas kernels, back_block(): pl.pallas_call(back_kernel, grid=(width // cut,), in_specs=[pl.BlockSpec(...  12.7 us
    pallas_call x1, Pallas kernels, outer_terms(): pl.pallas_call(outer_kernel, grid=(width // cut,), in_specs=[pl.BlockSpec...  12.3 us
  transfers between devices with their start and end apart: 36, of which 19 were waited for; matrix products, arithmetic and copies ran while one was open for 3% of the time, Pallas kernels for 8%

commit v1 on v0

--- a/solution.py
+++ b/solution.py
@@ -56,7 +56,7 @@
     wide = width // halves
     loads = [
         pltpu.make_async_copy(
-            weights.at[:, pl.ds(c * cut, cut), :], held.at[:, pl.ds(c * cut, cut), :], loaded.at[c]
+            weights.at[pl.ds(c * cut, cut), :], held.at[pl.ds(c * cut, cut), :], loaded.at[c]
         )
         for c in range(width // cut)
     ]
@@ -88,11 +88,12 @@
             loads[c].wait()
             here = pl.ds(c * cut, cut)
             x, dy = flat_x[:, here], flat_dy[:, here]
-            sums[0] += jnp.dot(x, held[0, here, :], preferred_element_type=F32)
-            sums[1] += jnp.dot(x, held[1, here, :], preferred_element_type=F32)
-            sums[2] += jnp.dot(dy, held[2, here, :], preferred_element_type=F32)
-
-    hidden[...], slopes[:, :half], slopes[:, half:] = activations(sums[0], sums[1], sums[2])
+            sums[:, :2 * half] += jnp.dot(x, held[here, :2 * half], preferred_element_type=F32)
+            sums[:, 2 * half:] += jnp.dot(dy, held[here, 2 * half:], preferred_element_type=F32)
+
+    hidden[...], slopes[:, :half], slopes[:, half:] = activations(
+        sums[:, :half], sums[:, half:2 * half], sums[:, 2 * half:]
+    )
     for keep in keeps:
         keep.wait()
 
@@ -100,7 +101,7 @@
 def expert_block(pieces, weights, capacity):
     counts = [p.shape[0] // (2 * capacity) for p in pieces]
     rows = sum(counts) * capacity
-    width, half = weights.shape[1:]
+    width, half = weights.shape[0], weights.shape[1] // 3
     anywhere, whole = pl.BlockSpec(memory_space=pl.ANY), pl.BlockSpec()
     return pl.pallas_call(
         functools.partial(expert_kernel, counts, capacity),
@@ -115,7 +116,7 @@
         scratch_shapes=[
             pltpu.VMEM((rows, width), BF16),
             pltpu.VMEM((rows, width), BF16),
-            pltpu.VMEM((3, rows, half), F32),
+            pltpu.VMEM((rows, 3 * half), F32),
             pltpu.VMEM(weights.shape, BF16),
             pltpu.SemaphoreType.DMA((2, 2)),
             pltpu.SemaphoreType.DMA((width // 1024,)),
@@ -129,29 +130,27 @@
 
 
 def back_kernel(slopes, weights, *backs):
-    half = weights.shape[2]
-    value = lax.dot_general(slopes[:, :half], weights[0], INNER, preferred_element_type=F32)
-    value += lax.dot_general(slopes[:, half:], weights[1], INNER, preferred_element_type=F32)
-    value = value.astype(BF16)
+    value = lax.dot_general(slopes[...], weights[...], INNER, preferred_element_type=F32).astype(BF16)
     rows = slopes.shape[0] // 4
     for i, back in enumerate(backs):
         back[...] = value[i * rows:(i + 1) * rows]
 
 
 def back_block(slopes, weights):
-    rows, (width, half), cut = slopes.shape[0], weights.shape[1:], 1024
+    rows, both = slopes.shape
+    width, cut = weights.shape[0], 1024
     return pl.pallas_call(
         back_kernel,
         grid=(width // cut,),
         in_specs=[
-            pl.BlockSpec((rows, 2 * half), lambda k: (0, 0)),
-            pl.BlockSpec((2, cut, half), lambda k: (0, k, 0)),
+            pl.BlockSpec((rows, both), lambda k: (0, 0)),
+            pl.BlockSpec((cut, both), lambda k: (k, 0)),
         ],
         out_specs=[pl.BlockSpec((rows // 4, cut), lambda k: (0, k))] * 4,
         out_shape=[jax.ShapeDtypeStruct((rows // 4, width), BF16)] * 4,
         compiler_params=pltpu.CompilerParams(vmem_limit_bytes=VMEM_BYTES),
         cost_estimate=pl.CostEstimate(
-            flops=4 * rows * width * half, bytes_accessed=9 * 2**20, transcendentals=0
+            flops=2 * rows * width * both, bytes_accessed=9 * 2**20, transcendentals=0
         ),
     )(slopes, weights)
 
@@ -214,8 +213,8 @@
 
     blocks = [block(s) for s in range(zs)]
     here = {0: blocks[0]}
-    shards = lax.optimization_barrier((w_gate, w_up, w_down, blocks[4]))[:3]
-    weights = lax.all_gather(jnp.concatenate(shards, 0), "dp", axis=1, tiled=True)
+    shards = lax.optimization_barrier((w_gate[0], w_up[0], w_down[0], blocks[7]))[:3]
+    weights = lax.all_gather(jnp.concatenate(shards, 1), "dp", axis=0, tiled=True)
 
     def round_of(sends, steps, *more):
         outs = []

time: 280 us -> 282 us (level)
  starting transfers between devices: 64.1 us -> 67.5 us
    ppermute x8, starting transfers between devices: 16.4 us -> 23.9 us  [home(): return lax.ppermute(homes[s], ('pipe', 'expert'), route)]
    ppermute x25, starting transfers between devices: 44.7 us -> 40.5 us  [moved(): lax.ppermute(block, 'expert', [(i, place(i)) for i in range(lax.axis_size...]
  transfers between devices with their start and end apart: 36 -> 36, of which waited for: 19 -> 18; matrix products, arithmetic and copies ran while one was open for 3% -> 3% of each run, Pallas kernels for 8% -> 8%
where the time goes in v1:
time: 282 us; the launch traced here: 281 us
  waiting for transfers between devices  136 us (48%)
  starting transfers between devices  67.5 us (24%)
  Pallas kernels  41.2 us (15%)
  between operations  14.8 us (5%)
  other arithmetic  11.2 us (4%)
  matrix products  6.37 us (2%)
  local copies, waits for them, and re-layouts  4.6 us (2%)
    ppermute x25, waiting for transfers between devices, moved(): lax.ppermute(block, 'expert', [(i, place(i)) for i in range(lax.axis_size...  94.3 us
    ppermute x8, waiting for transfers between devices, home(): return lax.ppermute(homes[s], ('pipe', 'expert'), route)  40.7 us
    ppermute x25, starting transfers between devices, moved(): lax.ppermute(block, 'expert', [(i, place(i)) for i in range(lax.axis_size...  40.5 us
    ppermute x8, starting transfers between devices, home(): return lax.ppermute(homes[s], ('pipe', 'expert'), route)  23.9 us
    pallas_call x2, Pallas kernels, expert_block(): pl.pallas_call(functools.partial(expert_kernel, counts, capacity), in_spe...  16.8 us
    pallas_call x1, Pallas kernels, outer_terms(): pl.pallas_call(outer_kernel, grid=(width // cut,), in_specs=[pl.BlockSpec...  12.3 us
    pallas_call x2, Pallas kernels, back_block(): pl.pallas_call(back_kernel, grid=(width // cut,), in_specs=[pl.BlockSpec(...  12 us
  transfers between devices with their start and end apart: 36, of which 18 were waited for; matrix products, arithmetic and copies ran while one was open for 3% of the time, Pallas kernels for 8%

profile of v1, /device:TPU:1, one launch (start us, length us, event | category | flops | bytes accessed | tf_op | source)
XLA Modules:
  0.0 281.4 jit_solution(12430357155925980991)
XLA Ops:
  14.6 6.5 %collective-permute-start.2 = (bf16[64,4096]{1,0:T(8,128)(2,1)S(1)}, bf16[64,4096]{1,0:T(8,128)(2,1)S(1)}, u32[]{:S(2)}, u32[]{:S(2)}) collective-permute-start(bf16[64,4096]{1,0:T(8,128)(2,1)S(1)} %convolution_convert_fusion.7), channel_id=1, source_target_pairs={{0,112},{4,116},{8,120},{12,124},{16,0},{20,4},{24,8},{28,12},{32,... | collective-permute-start | bytes 1572872 | tf_op jit(solution)/shard_map/ppermute | solution.py:35
  25.2 10.2 %collective-permute-done.1 = bf16[64,4096]{1,0:T(8,128)(2,1)S(1)} collective-permute-done((bf16[64,4096]{1,0:T(8,128)(2,1)S(1)}, bf16[64,4096]{1,0:T(8,128)(2,1)S(1)}, u32[]{:S(2)}, u32[]{:S(2)}) %collective-permute-start.1) | collective-permute-done | bytes 524320 | tf_op jit(solution)/shard_map/ppermute | solution.py:35
  35.5 2.8 %collective-permute-start.5 = (bf16[64,4096]{1,0:T(8,128)(2,1)S(1)}, bf16[64,4096]{1,0:T(8,128)(2,1)S(1)}, u32[]{:S(2)}, u32[]{:S(2)}) collective-permute-start(bf16[64,4096]{1,0:T(8,128)(2,1)S(1)} %pad_maximum_fusion.3), channel_id=1, source_target_pairs={{0,8},{4,12},{8,0},{12,4},{16,24},{20,28},{24,16},{28,20},{32,40},... | collective-permute-start | bytes 1572872 | tf_op jit(solution)/shard_map/ppermute | solution.py:35
  39.5 3.6 %collective-permute-start.7 = (bf16[64,4096]{1,0:T(8,128)(2,1)S(1)}, bf16[64,4096]{1,0:T(8,128)(2,1)S(1)}, u32[]{:S(2)}, u32[]{:S(2)}) collective-permute-start(bf16[64,4096]{1,0:T(8,128)(2,1)S(1)} %convolution_convert_fusion.5), channel_id=1, source_target_pairs={{0,96},{4,100},{8,104},{12,108},{16,112},{20,116},{24,120},{28,124... | collective-permute-start | bytes 1572872 | tf_op jit(solution)/shard_map/ppermute | solution.py:35
  43.5 16.6 %collective-permute-done.3.refs_2_ = bf16[64,4096]{1,0:T(8,128)(2,1)S(1)} collective-permute-done((bf16[64,4096]{1,0:T(8,128)(2,1)S(1)}, bf16[64,4096]{1,0:T(8,128)(2,1)S(1)}, u32[]{:S(2)}, u32[]{:S(2)}) %collective-permute-start.3) | collective-permute-done | bytes 524320 | tf_op jit(solution)/shard_map/ppermute | solution.py:35
  60.2 2.2 collective-permute-done.4.refs_4_
  62.3 2.5 collective-permute-done.6
  65.1 2.9 %collective-permute-start.10 = (bf16[96,4096]{1,0:T(8,128)(2,1)S(1)}, bf16[96,4096]{1,0:T(8,128)(2,1)S(1)}, u32[]{:S(2)}, u32[]{:S(2)}) collective-permute-start(bf16[96,4096]{1,0:T(8,128)(2,1)S(1)} %get-tuple-element.203), channel_id=1, source_target_pairs={{0,8},{4,12},{8,0},{12,4},{16,24},{20,28},{24,16},{28,20},{32,40},... | collective-permute-start | bytes 2359304 | tf_op jit(solution)/shard_map/ppermute | solution.py:35
  68.9 4.5 %collective-permute-start.12 = (bf16[64,4096]{1,0:T(8,128)(2,1)S(1)}, bf16[64,4096]{1,0:T(8,128)(2,1)S(1)}, u32[]{:S(2)}, u32[]{:S(2)}) collective-permute-start(bf16[64,4096]{1,0:T(8,128)(2,1)S(1)} %convolution_convert_fusion.3), channel_id=1, source_target_pairs={{0,80},{4,84},{8,88},{12,92},{16,96},{20,100},{24,104},{28,108},{3... | collective-permute-start | bytes 1572872 | tf_op jit(solution)/shard_map/ppermute | solution.py:35
  73.3 31.7 %collective-permute-done.11 = bf16[64,4096]{1,0:T(8,128)(2,1)S(1)} collective-permute-done((bf16[64,4096]{1,0:T(8,128)(2,1)S(1)}, bf16[64,4096]{1,0:T(8,128)(2,1)S(1)}, u32[]{:S(2)}, u32[]{:S(2)}) %collective-permute-start.11) | collective-permute-done | bytes 524320 | tf_op jit(solution)/shard_map/ppermute | solution.py:35
  111.1 3.9 %collective-permute-start.16 = (bf16[64,4096]{1,0:T(8,128)(2,1)}, bf16[64,4096]{1,0:T(8,128)(2,1)S(1)}, u32[]{:S(2)}, u32[]{:S(2)}) collective-permute-start(bf16[64,4096]{1,0:T(8,128)(2,1)} %convolution_convert_fusion.2), channel_id=1, source_target_pairs={{0,64},{4,68},{8,72},{12,76},{16,80},{20,84},{24,88},{28,92},{32,9... | collective-permute-start | bytes 1572872 | tf_op jit(solution)/shard_map/ppermute | solution.py:35
  115.0 9.9 %shard_map.102 = (bf16[320,4096]{1,0:T(8,128)(2,1)}, bf16[320,4096]{1,0:T(8,128)(2,1)}, bf16[320,384]{1,0:T(8,128)(2,1)}, bf16[320,768]{1,0:T(8,128)(2,1)}) custom-call(bf16[64,4096]{1,0:T(8,128)(2,1)} %copy-done, bf16[96,4096]{1,0:T(8,128)(2,1)} %copy-done.2, bf16[64,4096]{1,0:T(8,128)(2,1)} %copy-done.13, bf16[96,4096]{1,0:T(8,128)(2,1)} %copy-done.6, ...), custom_call_target="tpu_custom_call" | custom-call | flops 3019898880 | bytes 20971520 | tf_op jit(solution)/shard_map/pallas_call | solution.py:106
  124.9 5.8 %collective-permute-done.15.refs_6_ = bf16[64,4096]{1,0:T(8,128)(2,1)} collective-permute-done((bf16[64,4096]{1,0:T(8,128)(2,1)}, bf16[64,4096]{1,0:T(8,128)(2,1)}, u32[]{:S(2)}, u32[]{:S(2)}) %collective-permute-start.15) | collective-permute-done | bytes 524320 | tf_op jit(solution)/shard_map/ppermute | solution.py:35
  130.7 3.2 %collective-permute-done.14.refs_4_ = bf16[64,4096]{1,0:T(8,128)(2,1)S(1)} collective-permute-done((bf16[64,4096]{1,0:T(8,128)(2,1)}, bf16[64,4096]{1,0:T(8,128)(2,1)S(1)}, u32[]{:S(2)}, u32[]{:S(2)}) %collective-permute-start.14) | collective-permute-done | bytes 524320 | tf_op jit(solution)/shard_map/ppermute | solution.py:35
  134.0 2.3 collective-permute-start.19
  136.3 1.7 collective-permute-start.18
  138.0 6.2 %shard_map.103 = (bf16[80,4096]{1,0:T(8,128)(2,1)}, bf16[80,4096]{1,0:T(8,128)(2,1)}, bf16[80,4096]{1,0:T(8,128)(2,1)}, bf16[80,4096]{1,0:T(8,128)(2,1)}) custom-call(bf16[320,768]{1,0:T(8,128)(2,1)} %get-tuple-element.149.slopes.slopes_early, bf16[4096,1152]{1,0:T(8,128)(2,1)} %all-gather.2.cloned.1.call-done.refs_8_.weights), custom_call_target="tpu_custom_call" | custom-call | flops 2013265920 | bytes 9437184 | tf_op jit(solution)/shard_map/pallas_call | solution.py:142
  144.6 5.1 %collective-permute-done.18.refs_5_ = bf16[32,4096]{1,0:T(8,128)(2,1)S(1)} collective-permute-done((bf16[32,4096]{1,0:T(8,128)(2,1)S(1)}, bf16[32,4096]{1,0:T(8,128)(2,1)S(1)}, u32[]{:S(2)}, u32[]{:S(2)}) %collective-permute-start.18) | collective-permute-done | bytes 262176 | tf_op jit(solution)/shard_map/ppermute | solution.py:35
  150.4 6.9 %shard_map.104 = (bf16[192,4096]{1,0:T(8,128)(2,1)}, bf16[192,4096]{1,0:T(8,128)(2,1)}, bf16[192,384]{1,0:T(8,128)(2,1)}, bf16[192,768]{1,0:T(8,128)(2,1)}) custom-call(bf16[64,4096]{1,0:T(8,128)(2,1)} %copy-done.1, bf16[32,4096]{1,0:T(8,128)(2,1)} %copy-done.3, bf16[64,4096]{1,0:T(8,128)(2,1)} %copy-done.14, bf16[32,4096]{1,0:T(8,128)(2,1)} %copy-done.17, ...), custom_call_target="tpu_custom_call" | custom-call | flops 1811939328 | bytes 20971520 | tf_op jit(solution)/shard_map/pallas_call | solution.py:106
  157.3 12.3 %shard_map.105 = bf16[4096,1152]{1,0:T(8,128)(2,1)} custom-call(bf16[320,4096]{1,0:T(8,128)(2,1)} %get-tuple-element.145.x_early, bf16[192,4096]{1,0:T(8,128)(2,1)} %get-tuple-element.146.x_late, bf16[320,4096]{1,0:T(8,128)(2,1)} %get-tuple-element.147.dy_early, bf16[192,4096]{1,0:T(8,128)(2,1)} %get-tuple-element.148.dy_late, ...), custom_call_target="tpu_custom_call" | custom-call | tf_op jit(solution)/shard_map/pallas_call | solution.py:173
  174.0 3.0 %collective-permute-start = (f32[128]{0:T(128)S(1)}, f32[128]{0:T(128)S(1)}, u32[]{:S(2)}, u32[]{:S(2)}) collective-permute-start(f32[128]{0:T(128)S(1)} %get-tuple-element.174), channel_id=1, source_target_pairs={{0,128},{128,0},{1,129},{129,1},{2,130},{130,2},{3,131},{131,3},{4... | collective-permute-start | bytes 1544 | tf_op jit(solution)/shard_map/ppermute | solution.py:203
  177.8 5.9 %shard_map.106 = (bf16[48,4096]{1,0:T(8,128)(2,1)}, bf16[48,4096]{1,0:T(8,128)(2,1)}, bf16[48,4096]{1,0:T(8,128)(2,1)}, bf16[48,4096]{1,0:T(8,128)(2,1)}) custom-call(bf16[192,768]{1,0:T(8,128)(2,1)} %get-tuple-element.152.slopes_late.slopes, bf16[4096,1152]{1,0:T(8,128)(2,1)} %all-gather.2.cloned.1.call-done.refs_8_.weights), custom_call_target="tpu_custom_call" | custom-call | flops 1207959552 | bytes 9437184 | tf_op jit(solution)/shard_map/pallas_call | solution.py:142
  186.3 13.9 %collective-permute-done.22 = bf16[80,4096]{1,0:T(8,128)(2,1)S(1)} collective-permute-done((bf16[80,4096]{1,0:T(8,128)(2,1)S(1)}, bf16[80,4096]{1,0:T(8,128)(2,1)S(1)}, u32[]{:S(2)}, u32[]{:S(2)}) %collective-permute-start.22) | collective-permute-done | bytes 655392 | tf_op jit(solution)/shard_map/ppermute | solution.py:35
  201.3 2.2 collective-permute-start.25
  203.9 15.4 %collective-permute-start.26 = (bf16[32,4096]{1,0:T(8,128)(2,1)S(1)}, bf16[32,4096]{1,0:T(8,128)(2,1)S(1)}, u32[]{:S(2)}, u32[]{:S(2)}) collective-permute-start(bf16[32,4096]{1,0:T(8,128)(2,1)S(1)} %pad_maximum_fusion.8), channel_id=1, source_target_pairs={{0,224},{4,228},{8,232},{12,236},{16,240},{20,244},{24,248},{28,25... | collective-permute-start | bytes 786440 | tf_op jit(solution)/shard_map/ppermute | solution.py:277
  219.5 6.2 %collective-permute-done.26 = bf16[32,4096]{1,0:T(8,128)(2,1)S(1)} collective-permute-done((bf16[32,4096]{1,0:T(8,128)(2,1)S(1)}, bf16[32,4096]{1,0:T(8,128)(2,1)S(1)}, u32[]{:S(2)}, u32[]{:S(2)}) %collective-permute-start.26) | collective-permute-done | bytes 262176 | tf_op jit(solution)/shard_map/ppermute | solution.py:277
  225.7 3.2 %collective-permute-done.27 = bf16[32,4096]{1,0:T(8,128)(2,1)S(1)} collective-permute-done((bf16[32,4096]{1,0:T(8,128)(2,1)S(1)}, bf16[32,4096]{1,0:T(8,128)(2,1)S(1)}, u32[]{:S(2)}, u32[]{:S(2)}) %collective-permute-start.27) | collective-permute-done | bytes 262176 | tf_op jit(solution)/shard_map/ppermute | solution.py:277
  231.4 3.2 %collective-permute-start.30 = (bf16[32,4096]{1,0:T(8,128)(2,1)S(1)}, bf16[32,4096]{1,0:T(8,128)(2,1)S(1)}, u32[]{:S(2)}, u32[]{:S(2)}) collective-permute-start(bf16[32,4096]{1,0:T(8,128)(2,1)S(1)} %pad_maximum_fusion.13), channel_id=1, source_target_pairs={{0,208},{4,212},{8,216},{12,220},{16,224},{20,228},{24,232},{28,23... | collective-permute-start | bytes 786440 | tf_op jit(solution)/shard_map/ppermute | solution.py:277
  234.6 2.8 %collective-permute-start.31 = (bf16[32,4096]{1,0:T(8,128)(2,1)S(1)}, bf16[32,4096]{1,0:T(8,128)(2,1)S(1)}, u32[]{:S(2)}, u32[]{:S(2)}) collective-permute-start(bf16[32,4096]{1,0:T(8,128)(2,1)S(1)} %pad_maximum_fusion.14), channel_id=1, source_target_pairs={{0,192},{4,196},{8,200},{12,204},{16,208},{20,212},{24,216},{28,22... | collective-permute-start | bytes 786440 | tf_op jit(solution)/shard_map/ppermute | solution.py:277
  238.2 18.4 %collective-permute-done.30 = bf16[32,4096]{1,0:T(8,128)(2,1)S(1)} collective-permute-done((bf16[32,4096]{1,0:T(8,128)(2,1)S(1)}, bf16[32,4096]{1,0:T(8,128)(2,1)S(1)}, u32[]{:S(2)}, u32[]{:S(2)}) %collective-permute-start.30) | collective-permute-done | bytes 262176 | tf_op jit(solution)/shard_map/ppermute | solution.py:277
  256.7 12.4 %collective-permute-done.32 = bf16[32,4096]{1,0:T(8,128)(2,1)S(1)} collective-permute-done((bf16[32,4096]{1,0:T(8,128)(2,1)S(1)}, bf16[32,4096]{1,0:T(8,128)(2,1)S(1)}, u32[]{:S(2)}, u32[]{:S(2)}) %collective-permute-start.32) | collective-permute-done | bytes 262176 | tf_op jit(solution)/shard_map/ppermute | solution.py:277
  270.7 3.9 %bitcast_convert_fusion = (f32[1,1024,384]{2,1,0:T(8,128)}, f32[1,1024,384]{2,1,0:T(8,128)}, f32[1,1024,384]{2,1,0:T(8,128)}) fusion(bf16[1024,1152]{1,0:T(8,128)(2,1)} %reduce-scatter.2.cloned.1.call-done), kind=kLoop, calls=%fused_computation.15 | loop fusion | flops 1179648 | bytes 7077888 | tf_op jit(solution)/shard_map/broadcast_in_dim | solution.py:309
  (163 shorter events, 35.6 us)
Async XLA Ops:
  7.2 107.8 %all-gather.2.cloned.1.call-start = ((), (), s32[]{:S(2)}) async-start(), calls=%async_computation.1 | async-start | bytes 11796480 | tf_op jit(solution)/shard_map/all_gather | solution.py:217
  14.6 256.1 %reduce-scatter.2.cloned.1.call-start = ((), (), s32[]{:S(2)}) async-start(), calls=%async_computation.2 | async-start | bytes 11796480 | tf_op jit(solution)/shard_map/reduce_scatter | solution.py:288
  14.6 20.8 %collective-permute-start.2 = (bf16[64,4096]{1,0:T(8,128)(2,1)S(1)}, bf16[64,4096]{1,0:T(8,128)(2,1)S(1)}, u32[]{:S(2)}, u32[]{:S(2)}) collective-permute-start(bf16[64,4096]{1,0:T(8,128)(2,1)S(1)} %convolution_convert_fusion.7), channel_id=1, source_target_pairs={{0,112},{4,116},{8,120},{12,124},{16,0},{20,4},{24,8},{28,12},{32,... | collective-permute-start | bytes 1572872 | tf_op jit(solution)/shard_map/ppermute | solution.py:35
  21.6 13.8 %collective-permute-start.1 = (bf16[64,4096]{1,0:T(8,128)(2,1)S(1)}, bf16[64,4096]{1,0:T(8,128)(2,1)S(1)}, u32[]{:S(2)}, u32[]{:S(2)}) collective-permute-start(bf16[64,4096]{1,0:T(8,128)(2,1)S(1)} %convolution_convert_fusion.8), channel_id=1, source_target_pairs={{0,16},{4,20},{8,24},{12,28},{16,32},{20,36},{24,40},{28,44},{32,4... | collective-permute-start | bytes 1572872 | tf_op jit(solution)/shard_map/ppermute | solution.py:35
  35.5 24.6 %collective-permute-start.5 = (bf16[64,4096]{1,0:T(8,128)(2,1)S(1)}, bf16[64,4096]{1,0:T(8,128)(2,1)S(1)}, u32[]{:S(2)}, u32[]{:S(2)}) collective-permute-start(bf16[64,4096]{1,0:T(8,128)(2,1)S(1)} %pad_maximum_fusion.3), channel_id=1, source_target_pairs={{0,8},{4,12},{8,0},{12,4},{16,24},{20,28},{24,16},{28,20},{32,40},... | collective-permute-start | bytes 1572872 | tf_op jit(solution)/shard_map/ppermute | solution.py:35
  38.4 24.0 %collective-permute-start.4 = (bf16[64,4096]{1,0:T(8,128)(2,1)S(1)}, bf16[64,4096]{1,0:T(8,128)(2,1)S(1)}, u32[]{:S(2)}, u32[]{:S(2)}) collective-permute-start(bf16[64,4096]{1,0:T(8,128)(2,1)S(1)} %pad_maximum_fusion.3), channel_id=1, source_target_pairs={{0,12},{4,8},{8,4},{12,0},{16,28},{20,24},{24,20},{28,16},{32,44},... | collective-permute-start | bytes 1572872 | tf_op jit(solution)/shard_map/ppermute | solution.py:35
  39.3 20.9 %collective-permute-start.3 = (bf16[64,4096]{1,0:T(8,128)(2,1)S(1)}, bf16[64,4096]{1,0:T(8,128)(2,1)S(1)}, u32[]{:S(2)}, u32[]{:S(2)}) collective-permute-start(bf16[64,4096]{1,0:T(8,128)(2,1)S(1)} %pad_maximum_fusion.2.refs_0_), channel_id=1, source_target_pairs={{0,4},{4,0},{8,12},{12,8},{16,20},{20,16},{24,28},{28,24},{32,36},... | collective-permute-start | bytes 1572872 | tf_op jit(solution)/shard_map/ppermute | solution.py:35
  39.4 25.5 %collective-permute-start.6 = (bf16[64,4096]{1,0:T(8,128)(2,1)S(1)}, bf16[64,4096]{1,0:T(8,128)(2,1)S(1)}, u32[]{:S(2)}, u32[]{:S(2)}) collective-permute-start(bf16[64,4096]{1,0:T(8,128)(2,1)S(1)} %convolution_convert_fusion.6), channel_id=1, source_target_pairs={{0,32},{4,36},{8,40},{12,44},{16,48},{20,52},{24,56},{28,60},{32,6... | collective-permute-start | bytes 1572872 | tf_op jit(solution)/shard_map/ppermute | solution.py:35
  39.5 25.4 %collective-permute-start.7 = (bf16[64,4096]{1,0:T(8,128)(2,1)S(1)}, bf16[64,4096]{1,0:T(8,128)(2,1)S(1)}, u32[]{:S(2)}, u32[]{:S(2)}) collective-permute-start(bf16[64,4096]{1,0:T(8,128)(2,1)S(1)} %convolution_convert_fusion.5), channel_id=1, source_target_pairs={{0,96},{4,100},{8,104},{12,108},{16,112},{20,116},{24,120},{28,124... | collective-permute-start | bytes 1572872 | tf_op jit(solution)/shard_map/ppermute | solution.py:35
  65.1 40.0 %collective-permute-start.10 = (bf16[96,4096]{1,0:T(8,128)(2,1)S(1)}, bf16[96,4096]{1,0:T(8,128)(2,1)S(1)}, u32[]{:S(2)}, u32[]{:S(2)}) collective-permute-start(bf16[96,4096]{1,0:T(8,128)(2,1)S(1)} %get-tuple-element.203), channel_id=1, source_target_pairs={{0,8},{4,12},{8,0},{12,4},{16,24},{20,28},{24,16},{28,20},{32,40},... | collective-permute-start | bytes 2359304 | tf_op jit(solution)/shard_map/ppermute | solution.py:35
  68.0 37.1 %collective-permute-start.9 = (bf16[96,4096]{1,0:T(8,128)(2,1)S(1)}, bf16[96,4096]{1,0:T(8,128)(2,1)S(1)}, u32[]{:S(2)}, u32[]{:S(2)}) collective-permute-start(bf16[96,4096]{1,0:T(8,128)(2,1)S(1)} %get-tuple-element.203), channel_id=1, source_target_pairs={{0,12},{4,8},{8,4},{12,0},{16,28},{20,24},{24,20},{28,16},{32,44},... | collective-permute-start | bytes 2359304 | tf_op jit(solution)/shard_map/ppermute | solution.py:35
  68.9 36.2 %collective-permute-start.8 = (bf16[96,4096]{1,0:T(8,128)(2,1)S(1)}, bf16[96,4096]{1,0:T(8,128)(2,1)S(1)}, u32[]{:S(2)}, u32[]{:S(2)}) collective-permute-start(bf16[96,4096]{1,0:T(8,128)(2,1)S(1)} %get-tuple-element.105.refs_1_), channel_id=1, source_target_pairs={{0,4},{4,0},{8,12},{12,8},{16,20},{20,16},{24,28},{28,24},{32,36},... | collective-permute-start | bytes 2359304 | tf_op jit(solution)/shard_map/ppermute | solution.py:35
  68.9 36.2 %collective-permute-start.11 = (bf16[64,4096]{1,0:T(8,128)(2,1)S(1)}, bf16[64,4096]{1,0:T(8,128)(2,1)S(1)}, u32[]{:S(2)}, u32[]{:S(2)}) collective-permute-start(bf16[64,4096]{1,0:T(8,128)(2,1)S(1)} %convolution_convert_fusion.4), channel_id=1, source_target_pairs={{0,48},{4,52},{8,56},{12,60},{16,64},{20,68},{24,72},{28,76},{32,8... | collective-permute-start | bytes 1572872 | tf_op jit(solution)/shard_map/ppermute | solution.py:35
  68.9 36.2 %collective-permute-start.12 = (bf16[64,4096]{1,0:T(8,128)(2,1)S(1)}, bf16[64,4096]{1,0:T(8,128)(2,1)S(1)}, u32[]{:S(2)}, u32[]{:S(2)}) collective-permute-start(bf16[64,4096]{1,0:T(8,128)(2,1)S(1)} %convolution_convert_fusion.3), channel_id=1, source_target_pairs={{0,80},{4,84},{8,88},{12,92},{16,96},{20,100},{24,104},{28,108},{3... | collective-permute-start | bytes 1572872 | tf_op jit(solution)/shard_map/ppermute | solution.py:35
  106.2 18.7 %collective-permute-start.13 = (bf16[64,4096]{1,0:T(8,128)(2,1)S(1)}, bf16[64,4096]{1,0:T(8,128)(2,1)S(1)}, u32[]{:S(2)}, u32[]{:S(2)}) collective-permute-start(bf16[64,4096]{1,0:T(8,128)(2,1)S(1)} %pad_maximum_fusion.4.refs_0_), channel_id=1, source_target_pairs={{0,4},{4,0},{8,12},{12,8},{16,20},{20,16},{24,28},{28,24},{32,36},... | collective-permute-start | bytes 1572872 | tf_op jit(solution)/shard_map/ppermute | solution.py:35
  108.6 22.1 %collective-permute-start.15 = (bf16[64,4096]{1,0:T(8,128)(2,1)}, bf16[64,4096]{1,0:T(8,128)(2,1)}, u32[]{:S(2)}, u32[]{:S(2)}) collective-permute-start(bf16[64,4096]{1,0:T(8,128)(2,1)} %pad_maximum_fusion.5), channel_id=1, source_target_pairs={{0,8},{4,12},{8,0},{12,4},{16,24},{20,28},{24,16},{28,20},{32,40},... | collective-permute-start | bytes 1572872 | tf_op jit(solution)/shard_map/ppermute | solution.py:35
  110.2 23.6 %collective-permute-start.14 = (bf16[64,4096]{1,0:T(8,128)(2,1)}, bf16[64,4096]{1,0:T(8,128)(2,1)S(1)}, u32[]{:S(2)}, u32[]{:S(2)}) collective-permute-start(bf16[64,4096]{1,0:T(8,128)(2,1)} %pad_maximum_fusion.5), channel_id=1, source_target_pairs={{0,12},{4,8},{8,4},{12,0},{16,28},{20,24},{24,20},{28,16},{32,44},... | collective-permute-start | bytes 1572872 | tf_op jit(solution)/shard_map/ppermute | solution.py:35
  111.1 22.7 %collective-permute-start.16 = (bf16[64,4096]{1,0:T(8,128)(2,1)}, bf16[64,4096]{1,0:T(8,128)(2,1)S(1)}, u32[]{:S(2)}, u32[]{:S(2)}) collective-permute-start(bf16[64,4096]{1,0:T(8,128)(2,1)} %convolution_convert_fusion.2), channel_id=1, source_target_pairs={{0,64},{4,68},{8,72},{12,76},{16,80},{20,84},{24,88},{28,92},{32,9... | collective-permute-start | bytes 1572872 | tf_op jit(solution)/shard_map/ppermute | solution.py:35
  133.9 10.2 %collective-permute-start.17 = (bf16[32,4096]{1,0:T(8,128)(2,1)S(1)}, bf16[32,4096]{1,0:T(8,128)(2,1)S(1)}, u32[]{:S(2)}, u32[]{:S(2)}) collective-permute-start(bf16[32,4096]{1,0:T(8,128)(2,1)S(1)} %pad_maximum_fusion.6.refs_1_), channel_id=1, source_target_pairs={{0,4},{4,0},{8,12},{12,8},{16,20},{20,16},{24,28},{28,24},{32,36},... | collective-permute-start | bytes 786440 | tf_op jit(solution)/shard_map/ppermute | solution.py:35
  134.0 10.6 %collective-permute-start.19 = (bf16[32,4096]{1,0:T(8,128)(2,1)S(1)}, bf16[32,4096]{1,0:T(8,128)(2,1)S(1)}, u32[]{:S(2)}, u32[]{:S(2)}) collective-permute-start(bf16[32,4096]{1,0:T(8,128)(2,1)S(1)} %pad_maximum_fusion.7), channel_id=1, source_target_pairs={{0,8},{4,12},{8,0},{12,4},{16,24},{20,28},{24,16},{28,20},{32,40},... | collective-permute-start | bytes 786440 | tf_op jit(solution)/shard_map/ppermute | solution.py:35
  136.3 13.4 %collective-permute-start.18 = (bf16[32,4096]{1,0:T(8,128)(2,1)S(1)}, bf16[32,4096]{1,0:T(8,128)(2,1)S(1)}, u32[]{:S(2)}, u32[]{:S(2)}) collective-permute-start(bf16[32,4096]{1,0:T(8,128)(2,1)S(1)} %pad_maximum_fusion.7), channel_id=1, source_target_pairs={{0,12},{4,8},{8,4},{12,0},{16,28},{20,24},{24,20},{28,16},{32,44},... | collective-permute-start | bytes 786440 | tf_op jit(solution)/shard_map/ppermute | solution.py:35
  170.7 14.1 %collective-permute-start.20 = (bf16[80,4096]{1,0:T(8,128)(2,1)S(1)}, bf16[80,4096]{1,0:T(8,128)(2,1)S(1)}, u32[]{:S(2)}, u32[]{:S(2)}) collective-permute-start(bf16[80,4096]{1,0:T(8,128)(2,1)S(1)} %copy-done.24), channel_id=1, source_target_pairs={{0,4},{4,0},{8,12},{12,8},{16,20},{20,16},{24,28},{28,24},{32,36},... | collective-permute-start | bytes 1966088 | tf_op jit(solution)/shard_map/ppermute | solution.py:35
  170.9 15.3 %collective-permute-start.21 = (bf16[80,4096]{1,0:T(8,128)(2,1)S(1)}, bf16[80,4096]{1,0:T(8,128)(2,1)S(1)}, u32[]{:S(2)}, u32[]{:S(2)}) collective-permute-start(bf16[80,4096]{1,0:T(8,128)(2,1)S(1)} %copy-done.23), channel_id=1, source_target_pairs={{0,12},{4,8},{8,4},{12,0},{16,28},{20,24},{24,20},{28,16},{32,44},... | collective-permute-start | bytes 1966088 | tf_op jit(solution)/shard_map/ppermute | solution.py:35
  172.6 27.6 %collective-permute-start.22 = (bf16[80,4096]{1,0:T(8,128)(2,1)S(1)}, bf16[80,4096]{1,0:T(8,128)(2,1)S(1)}, u32[]{:S(2)}, u32[]{:S(2)}) collective-permute-start(bf16[80,4096]{1,0:T(8,128)(2,1)S(1)} %copy-done.22), channel_id=1, source_target_pairs={{0,8},{4,12},{8,0},{12,4},{16,24},{20,28},{24,16},{28,20},{32,40},... | collective-permute-start | bytes 1966088 | tf_op jit(solution)/shard_map/ppermute | solution.py:35
  200.2 28.6 %collective-permute-start.23 = (bf16[48,4096]{1,0:T(8,128)(2,1)}, bf16[48,4096]{1,0:T(8,128)(2,1)S(1)}, u32[]{:S(2)}, u32[]{:S(2)}) collective-permute-start(bf16[48,4096]{1,0:T(8,128)(2,1)} %get-tuple-element.157), channel_id=1, source_target_pairs={{0,4},{4,0},{8,12},{12,8},{16,20},{20,16},{24,28},{28,24},{32,36},... | collective-permute-start | bytes 1179656 | tf_op jit(solution)/shard_map/ppermute | solution.py:35
  200.2 28.6 %collective-permute-start.24 = (bf16[48,4096]{1,0:T(8,128)(2,1)}, bf16[48,4096]{1,0:T(8,128)(2,1)S(1)}, u32[]{:S(2)}, u32[]{:S(2)}) collective-permute-start(bf16[48,4096]{1,0:T(8,128)(2,1)} %get-tuple-element.158), channel_id=1, source_target_pairs={{0,12},{4,8},{8,4},{12,0},{16,28},{20,24},{24,20},{28,16},{32,44},... | collective-permute-start | bytes 1179656 | tf_op jit(solution)/shard_map/ppermute | solution.py:35
  201.3 27.5 %collective-permute-start.25 = (bf16[48,4096]{1,0:T(8,128)(2,1)}, bf16[48,4096]{1,0:T(8,128)(2,1)S(1)}, u32[]{:S(2)}, u32[]{:S(2)}) collective-permute-start(bf16[48,4096]{1,0:T(8,128)(2,1)} %get-tuple-element.159), channel_id=1, source_target_pairs={{0,8},{4,12},{8,0},{12,4},{16,24},{20,28},{24,16},{28,20},{32,40},... | collective-permute-start | bytes 1179656 | tf_op jit(solution)/shard_map/ppermute | solution.py:35
  203.9 21.7 %collective-permute-start.26 = (bf16[32,4096]{1,0:T(8,128)(2,1)S(1)}, bf16[32,4096]{1,0:T(8,128)(2,1)S(1)}, u32[]{:S(2)}, u32[]{:S(2)}) collective-permute-start(bf16[32,4096]{1,0:T(8,128)(2,1)S(1)} %pad_maximum_fusion.8), channel_id=1, source_target_pairs={{0,224},{4,228},{8,232},{12,236},{16,240},{20,244},{24,248},{28,25... | collective-permute-start | bytes 786440 | tf_op jit(solution)/shard_map/ppermute | solution.py:277
  230.6 38.6 %collective-permute-start.33 = (bf16[32,4096]{1,0:T(8,128)(2,1)S(1)}, bf16[32,4096]{1,0:T(8,128)(2,1)S(1)}, u32[]{:S(2)}, u32[]{:S(2)}) collective-permute-start(bf16[32,4096]{1,0:T(8,128)(2,1)S(1)} %pad_maximum_fusion.12), channel_id=1, source_target_pairs={{0,144},{4,148},{8,152},{12,156},{16,160},{20,164},{24,168},{28,17... | collective-permute-start | bytes 786440 | tf_op jit(solution)/shard_map/ppermute | solution.py:277
  231.4 25.3 %collective-permute-start.30 = (bf16[32,4096]{1,0:T(8,128)(2,1)S(1)}, bf16[32,4096]{1,0:T(8,128)(2,1)S(1)}, u32[]{:S(2)}, u32[]{:S(2)}) collective-permute-start(bf16[32,4096]{1,0:T(8,128)(2,1)S(1)} %pad_maximum_fusion.13), channel_id=1, source_target_pairs={{0,208},{4,212},{8,216},{12,220},{16,224},{20,228},{24,232},{28,23... | collective-permute-start | bytes 786440 | tf_op jit(solution)/shard_map/ppermute | solution.py:277
  234.6 22.1 %collective-permute-start.31 = (bf16[32,4096]{1,0:T(8,128)(2,1)S(1)}, bf16[32,4096]{1,0:T(8,128)(2,1)S(1)}, u32[]{:S(2)}, u32[]{:S(2)}) collective-permute-start(bf16[32,4096]{1,0:T(8,128)(2,1)S(1)} %pad_maximum_fusion.14), channel_id=1, source_target_pairs={{0,192},{4,196},{8,200},{12,204},{16,208},{20,212},{24,216},{28,22... | collective-permute-start | bytes 786440 | tf_op jit(solution)/shard_map/ppermute | solution.py:277
  237.5 31.6 %collective-permute-start.32 = (bf16[32,4096]{1,0:T(8,128)(2,1)S(1)}, bf16[32,4096]{1,0:T(8,128)(2,1)S(1)}, u32[]{:S(2)}, u32[]{:S(2)}) collective-permute-start(bf16[32,4096]{1,0:T(8,128)(2,1)S(1)} %pad_maximum_fusion.15), channel_id=1, source_target_pairs={{0,176},{4,180},{8,184},{12,188},{16,192},{20,196},{24,200},{28,20... | collective-permute-start | bytes 786440 | tf_op jit(solution)/shard_map/ppermute | solution.py:277
  (29 other events, 305.7 us)
Sparse Core Ops, SparseCore 0:
  14.7 98.3 all-gather.1
  169.8 98.4 reduce-scatter.1

commit v2 on v1

--- a/solution.py
+++ b/solution.py
@@ -291,12 +291,13 @@
     summed(early[4:], came, early_steps)
     back_late = [b0, b1, b2, b3]
     came = returned(back_late)
-    near = {s: home(s) for s in (2, 6)}
-    came = list(lax.optimization_barrier((*came, near[2], near[6], *[homes[s] for s in (0, 1, 7)])))
-    near = dict(zip((2, 6), came[3:5]))
-    homes.update(zip((0, 1, 7), came[5:8]))
+    near_steps = (2, 6, 1, 7)
+    near = [home(s) for s in near_steps]
+    *came, rows_here = lax.optimization_barrier((*came, *near, homes[0]))
+    near = dict(zip(near_steps, came[3:]))
+    homes[0] = rows_here
     summed(back_late, came[:3], late_steps)
-    homes = {s: home(s) for s in (3, 5, 4, 1, 7, 0)} | near
+    homes = {s: home(s) for s in (4, 3, 5, 0)} | near
     summed_rows = jnp.concatenate([homes[s] for s in range(zs)], 0)
     slots = jnp.arange(2 * zs * capacity, dtype=jnp.int32)
     combine = (slots[None, :] == other_column.astype(jnp.int32)[:, None]).astype(BF16)

time: 282 us -> 287 us (1.018)
  waiting for transfers between devices: 136 us -> 144 us
    ppermute x8, waiting for transfers between devices: 40.7 us -> 48.5 us  [home(): return lax.ppermute(homes[s], ('pipe', 'expert'), route)]
where the time goes in v2:
time: 287 us
  waiting for transfers between devices  144 us (50%)
  starting transfers between devices  65.2 us (23%)
  Pallas kernels  41.2 us (14%)
  between operations  14.8 us (5%)
  other arithmetic  11.2 us (4%)
  matrix products  6.37 us (2%)
  local copies, waits for them, and re-layouts  4.6 us (2%)
    ppermute x25, waiting for transfers between devices, moved(): lax.ppermute(block, 'expert', [(i, place(i)) for i in range(lax.axis_size...  94.3 us
    ppermute x8, waiting for transfers between devices, home(): return lax.ppermute(homes[s], ('pipe', 'expert'), route)  48.5 us
    ppermute x25, starting transfers between devices, moved(): lax.ppermute(block, 'expert', [(i, place(i)) for i in range(lax.axis_size...  40.5 us
    ppermute x8, starting transfers between devices, home(): return lax.ppermute(homes[s], ('pipe', 'expert'), route)  21.6 us
    pallas_call x2, Pallas kernels, expert_block(): pl.pallas_call(functools.partial(expert_kernel, counts, capacity), in_spe...  16.8 us
    pallas_call x1, Pallas kernels, outer_terms(): pl.pallas_call(outer_kernel, grid=(width // cut,), in_specs=[pl.BlockSpec...  12.3 us
    pallas_call x2, Pallas kernels, back_block(): pl.pallas_call(back_kernel, grid=(width // cut,), in_specs=[pl.BlockSpec(...  12 us
  transfers between devices with their start and end apart: 36, of which 18 were waited for; matrix products, arithmetic and copies ran while one was open for 3% of the time, Pallas kernels for 8%

profile of v2, /device:TPU:1, one launch (start us, length us, event | category | flops | bytes accessed | tf_op | source)
XLA Modules:
  0.0 286.9 jit_solution(1198679177165799101)
XLA Ops:
  14.6 6.5 %collective-permute-start.2 = (bf16[64,4096]{1,0:T(8,128)(2,1)S(1)}, bf16[64,4096]{1,0:T(8,128)(2,1)S(1)}, u32[]{:S(2)}, u32[]{:S(2)}) collective-permute-start(bf16[64,4096]{1,0:T(8,128)(2,1)S(1)} %convolution_convert_fusion.7), channel_id=1, source_target_pairs={{0,112},{4,116},{8,120},{12,124},{16,0},{20,4},{24,8},{28,12},{32,... | collective-permute-start | bytes 1572872 | tf_op jit(solution)/shard_map/ppermute | solution.py:35
  25.2 10.2 %collective-permute-done.1 = bf16[64,4096]{1,0:T(8,128)(2,1)S(1)} collective-permute-done((bf16[64,4096]{1,0:T(8,128)(2,1)S(1)}, bf16[64,4096]{1,0:T(8,128)(2,1)S(1)}, u32[]{:S(2)}, u32[]{:S(2)}) %collective-permute-start.1) | collective-permute-done | bytes 524320 | tf_op jit(solution)/shard_map/ppermute | solution.py:35
  35.5 2.8 collective-permute-start.5
  39.5 3.6 %collective-permute-start.7 = (bf16[64,4096]{1,0:T(8,128)(2,1)S(1)}, bf16[64,4096]{1,0:T(8,128)(2,1)S(1)}, u32[]{:S(2)}, u32[]{:S(2)}) collective-permute-start(bf16[64,4096]{1,0:T(8,128)(2,1)S(1)} %convolution_convert_fusion.5), channel_id=1, source_target_pairs={{0,96},{4,100},{8,104},{12,108},{16,112},{20,116},{24,120},{28,124... | collective-permute-start | bytes 1572872 | tf_op jit(solution)/shard_map/ppermute | solution.py:35
  43.5 16.6 %collective-permute-done.3.refs_2_ = bf16[64,4096]{1,0:T(8,128)(2,1)S(1)} collective-permute-done((bf16[64,4096]{1,0:T(8,128)(2,1)S(1)}, bf16[64,4096]{1,0:T(8,128)(2,1)S(1)}, u32[]{:S(2)}, u32[]{:S(2)}) %collective-permute-start.3) | collective-permute-done | bytes 524320 | tf_op jit(solution)/shard_map/ppermute | solution.py:35
  60.2 2.2 collective-permute-done.4.refs_4_
  62.3 2.5 collective-permute-done.6
  65.1 2.9 %collective-permute-start.10 = (bf16[96,4096]{1,0:T(8,128)(2,1)S(1)}, bf16[96,4096]{1,0:T(8,128)(2,1)S(1)}, u32[]{:S(2)}, u32[]{:S(2)}) collective-permute-start(bf16[96,4096]{1,0:T(8,128)(2,1)S(1)} %get-tuple-element.203), channel_id=1, source_target_pairs={{0,8},{4,12},{8,0},{12,4},{16,24},{20,28},{24,16},{28,20},{32,40},... | collective-permute-start | bytes 2359304 | tf_op jit(solution)/shard_map/ppermute | solution.py:35
  68.9 4.5 %collective-permute-start.12 = (bf16[64,4096]{1,0:T(8,128)(2,1)S(1)}, bf16[64,4096]{1,0:T(8,128)(2,1)S(1)}, u32[]{:S(2)}, u32[]{:S(2)}) collective-permute-start(bf16[64,4096]{1,0:T(8,128)(2,1)S(1)} %convolution_convert_fusion.3), channel_id=1, source_target_pairs={{0,80},{4,84},{8,88},{12,92},{16,96},{20,100},{24,104},{28,108},{3... | collective-permute-start | bytes 1572872 | tf_op jit(solution)/shard_map/ppermute | solution.py:35
  73.3 31.7 %collective-permute-done.11 = bf16[64,4096]{1,0:T(8,128)(2,1)S(1)} collective-permute-done((bf16[64,4096]{1,0:T(8,128)(2,1)S(1)}, bf16[64,4096]{1,0:T(8,128)(2,1)S(1)}, u32[]{:S(2)}, u32[]{:S(2)}) %collective-permute-start.11) | collective-permute-done | bytes 524320 | tf_op jit(solution)/shard_map/ppermute | solution.py:35
  111.1 3.9 %collective-permute-start.16 = (bf16[64,4096]{1,0:T(8,128)(2,1)}, bf16[64,4096]{1,0:T(8,128)(2,1)S(1)}, u32[]{:S(2)}, u32[]{:S(2)}) collective-permute-start(bf16[64,4096]{1,0:T(8,128)(2,1)} %convolution_convert_fusion.2), channel_id=1, source_target_pairs={{0,64},{4,68},{8,72},{12,76},{16,80},{20,84},{24,88},{28,92},{32,9... | collective-permute-start | bytes 1572872 | tf_op jit(solution)/shard_map/ppermute | solution.py:35
  115.0 9.9 %shard_map.102 = (bf16[320,4096]{1,0:T(8,128)(2,1)}, bf16[320,4096]{1,0:T(8,128)(2,1)}, bf16[320,384]{1,0:T(8,128)(2,1)}, bf16[320,768]{1,0:T(8,128)(2,1)}) custom-call(bf16[64,4096]{1,0:T(8,128)(2,1)} %copy-done, bf16[96,4096]{1,0:T(8,128)(2,1)} %copy-done.2, bf16[64,4096]{1,0:T(8,128)(2,1)} %copy-done.13, bf16[96,4096]{1,0:T(8,128)(2,1)} %copy-done.6, ...), custom_call_target="tpu_custom_call" | custom-call | flops 3019898880 | bytes 20971520 | tf_op jit(solution)/shard_map/pallas_call | solution.py:106
  124.9 5.8 %collective-permute-done.15.refs_6_ = bf16[64,4096]{1,0:T(8,128)(2,1)} collective-permute-done((bf16[64,4096]{1,0:T(8,128)(2,1)}, bf16[64,4096]{1,0:T(8,128)(2,1)}, u32[]{:S(2)}, u32[]{:S(2)}) %collective-permute-start.15) | collective-permute-done | bytes 524320 | tf_op jit(solution)/shard_map/ppermute | solution.py:35
  130.7 3.2 %collective-permute-done.14.refs_4_ = bf16[64,4096]{1,0:T(8,128)(2,1)S(1)} collective-permute-done((bf16[64,4096]{1,0:T(8,128)(2,1)}, bf16[64,4096]{1,0:T(8,128)(2,1)S(1)}, u32[]{:S(2)}, u32[]{:S(2)}) %collective-permute-start.14) | collective-permute-done | bytes 524320 | tf_op jit(solution)/shard_map/ppermute | solution.py:35
  134.0 2.3 collective-permute-start.19
  138.0 6.2 %shard_map.103 = (bf16[80,4096]{1,0:T(8,128)(2,1)}, bf16[80,4096]{1,0:T(8,128)(2,1)}, bf16[80,4096]{1,0:T(8,128)(2,1)}, bf16[80,4096]{1,0:T(8,128)(2,1)}) custom-call(bf16[320,768]{1,0:T(8,128)(2,1)} %get-tuple-element.149.slopes.slopes_early, bf16[4096,1152]{1,0:T(8,128)(2,1)} %all-gather.2.cloned.1.call-done.refs_8_.weights), custom_call_target="tpu_custom_call" | custom-call | flops 2013265920 | bytes 9437184 | tf_op jit(solution)/shard_map/pallas_call | solution.py:142
  144.6 5.1 %collective-permute-done.18.refs_5_ = bf16[32,4096]{1,0:T(8,128)(2,1)S(1)} collective-permute-done((bf16[32,4096]{1,0:T(8,128)(2,1)S(1)}, bf16[32,4096]{1,0:T(8,128)(2,1)S(1)}, u32[]{:S(2)}, u32[]{:S(2)}) %collective-permute-start.18) | collective-permute-done | bytes 262176 | tf_op jit(solution)/shard_map/ppermute | solution.py:35
  150.4 6.9 %shard_map.104 = (bf16[192,4096]{1,0:T(8,128)(2,1)}, bf16[192,4096]{1,0:T(8,128)(2,1)}, bf16[192,384]{1,0:T(8,128)(2,1)}, bf16[192,768]{1,0:T(8,128)(2,1)}) custom-call(bf16[64,4096]{1,0:T(8,128)(2,1)} %copy-done.1, bf16[32,4096]{1,0:T(8,128)(2,1)} %copy-done.3, bf16[64,4096]{1,0:T(8,128)(2,1)} %copy-done.14, bf16[32,4096]{1,0:T(8,128)(2,1)} %copy-done.17, ...), custom_call_target="tpu_custom_call" | custom-call | flops 1811939328 | bytes 20971520 | tf_op jit(solution)/shard_map/pallas_call | solution.py:106
  157.3 12.3 %shard_map.105 = bf16[4096,1152]{1,0:T(8,128)(2,1)} custom-call(bf16[320,4096]{1,0:T(8,128)(2,1)} %get-tuple-element.145.x_early, bf16[192,4096]{1,0:T(8,128)(2,1)} %get-tuple-element.146.x_late, bf16[320,4096]{1,0:T(8,128)(2,1)} %get-tuple-element.147.dy_early, bf16[192,4096]{1,0:T(8,128)(2,1)} %get-tuple-element.148.dy_late, ...), custom_call_target="tpu_custom_call" | custom-call | tf_op jit(solution)/shard_map/pallas_call | solution.py:173
  174.0 3.0 %collective-permute-start = (f32[128]{0:T(128)S(1)}, f32[128]{0:T(128)S(1)}, u32[]{:S(2)}, u32[]{:S(2)}) collective-permute-start(f32[128]{0:T(128)S(1)} %get-tuple-element.174), channel_id=1, source_target_pairs={{0,128},{128,0},{1,129},{129,1},{2,130},{130,2},{3,131},{131,3},{4... | collective-permute-start | bytes 1544 | tf_op jit(solution)/shard_map/ppermute | solution.py:203
  177.8 5.9 %shard_map.106 = (bf16[48,4096]{1,0:T(8,128)(2,1)}, bf16[48,4096]{1,0:T(8,128)(2,1)}, bf16[48,4096]{1,0:T(8,128)(2,1)}, bf16[48,4096]{1,0:T(8,128)(2,1)}) custom-call(bf16[192,768]{1,0:T(8,128)(2,1)} %get-tuple-element.152.slopes_late.slopes, bf16[4096,1152]{1,0:T(8,128)(2,1)} %all-gather.2.cloned.1.call-done.refs_8_.weights), custom_call_target="tpu_custom_call" | custom-call | flops 1207959552 | bytes 9437184 | tf_op jit(solution)/shard_map/pallas_call | solution.py:142
  186.3 13.9 %collective-permute-done.22 = bf16[80,4096]{1,0:T(8,128)(2,1)S(1)} collective-permute-done((bf16[80,4096]{1,0:T(8,128)(2,1)S(1)}, bf16[80,4096]{1,0:T(8,128)(2,1)S(1)}, u32[]{:S(2)}, u32[]{:S(2)}) %collective-permute-start.22) | collective-permute-done | bytes 655392 | tf_op jit(solution)/shard_map/ppermute | solution.py:35
  201.3 2.2 collective-permute-start.25
  203.9 15.4 %collective-permute-start.26 = (bf16[32,4096]{1,0:T(8,128)(2,1)S(1)}, bf16[32,4096]{1,0:T(8,128)(2,1)S(1)}, u32[]{:S(2)}, u32[]{:S(2)}) collective-permute-start(bf16[32,4096]{1,0:T(8,128)(2,1)S(1)} %pad_maximum_fusion.8), channel_id=1, source_target_pairs={{0,224},{4,228},{8,232},{12,236},{16,240},{20,244},{24,248},{28,25... | collective-permute-start | bytes 786440 | tf_op jit(solution)/shard_map/ppermute | solution.py:277
  219.5 7.5 %collective-permute-done.26 = bf16[32,4096]{1,0:T(8,128)(2,1)S(1)} collective-permute-done((bf16[32,4096]{1,0:T(8,128)(2,1)S(1)}, bf16[32,4096]{1,0:T(8,128)(2,1)S(1)}, u32[]{:S(2)}, u32[]{:S(2)}) %collective-permute-start.26) | collective-permute-done | bytes 262176 | tf_op jit(solution)/shard_map/ppermute | solution.py:277
  227.0 1.9 collective-permute-start.28
  228.9 5.6 %collective-permute-done.28 = bf16[32,4096]{1,0:T(8,128)(2,1)S(1)} collective-permute-done((bf16[32,4096]{1,0:T(8,128)(2,1)S(1)}, bf16[32,4096]{1,0:T(8,128)(2,1)S(1)}, u32[]{:S(2)}, u32[]{:S(2)}) %collective-permute-start.28) | collective-permute-done | bytes 262176 | tf_op jit(solution)/shard_map/ppermute | solution.py:277
  234.5 4.3 %collective-permute-done.29 = bf16[32,4096]{1,0:T(8,128)(2,1)S(1)} collective-permute-done((bf16[32,4096]{1,0:T(8,128)(2,1)S(1)}, bf16[32,4096]{1,0:T(8,128)(2,1)S(1)}, u32[]{:S(2)}, u32[]{:S(2)}) %collective-permute-start.29) | collective-permute-done | bytes 262176 | tf_op jit(solution)/shard_map/ppermute | solution.py:277
  239.6 2.9 collective-permute-start.32
  243.5 17.0 %collective-permute-done.31 = bf16[32,4096]{1,0:T(8,128)(2,1)S(1)} collective-permute-done((bf16[32,4096]{1,0:T(8,128)(2,1)S(1)}, bf16[32,4096]{1,0:T(8,128)(2,1)S(1)}, u32[]{:S(2)}, u32[]{:S(2)}) %collective-permute-start.31) | collective-permute-done | bytes 262176 | tf_op jit(solution)/shard_map/ppermute | solution.py:277
  260.6 14.0 %collective-permute-done.33 = bf16[32,4096]{1,0:T(8,128)(2,1)S(1)} collective-permute-done((bf16[32,4096]{1,0:T(8,128)(2,1)S(1)}, bf16[32,4096]{1,0:T(8,128)(2,1)S(1)}, u32[]{:S(2)}, u32[]{:S(2)}) %collective-permute-start.33) | collective-permute-done | bytes 262176 | tf_op jit(solution)/shard_map/ppermute | solution.py:277
  276.2 3.9 %bitcast_convert_fusion = (f32[1,1024,384]{2,1,0:T(8,128)}, f32[1,1024,384]{2,1,0:T(8,128)}, f32[1,1024,384]{2,1,0:T(8,128)}) fusion(bf16[1024,1152]{1,0:T(8,128)(2,1)} %reduce-scatter.2.cloned.1.call-done), kind=kLoop, calls=%fused_computation.15 | loop fusion | flops 1179648 | bytes 7077888 | tf_op jit(solution)/shard_map/broadcast_in_dim | solution.py:310
  (163 shorter events, 35.7 us)
Async XLA Ops:
  7.2 107.8 %all-gather.2.cloned.1.call-start = ((), (), s32[]{:S(2)}) async-start(), calls=%async_computation.1 | async-start | bytes 11796480 | tf_op jit(solution)/shard_map/all_gather | solution.py:217
  14.6 261.6 %reduce-scatter.2.cloned.1.call-start = ((), (), s32[]{:S(2)}) async-start(), calls=%async_computation.2 | async-start | bytes 11796480 | tf_op jit(solution)/shard_map/reduce_scatter | solution.py:288
  14.6 20.8 %collective-permute-start.2 = (bf16[64,4096]{1,0:T(8,128)(2,1)S(1)}, bf16[64,4096]{1,0:T(8,128)(2,1)S(1)}, u32[]{:S(2)}, u32[]{:S(2)}) collective-permute-start(bf16[64,4096]{1,0:T(8,128)(2,1)S(1)} %convolution_convert_fusion.7), channel_id=1, source_target_pairs={{0,112},{4,116},{8,120},{12,124},{16,0},{20,4},{24,8},{28,12},{32,... | collective-permute-start | bytes 1572872 | tf_op jit(solution)/shard_map/ppermute | solution.py:35
  21.6 13.8 %collective-permute-start.1 = (bf16[64,4096]{1,0:T(8,128)(2,1)S(1)}, bf16[64,4096]{1,0:T(8,128)(2,1)S(1)}, u32[]{:S(2)}, u32[]{:S(2)}) collective-permute-start(bf16[64,4096]{1,0:T(8,128)(2,1)S(1)} %convolution_convert_fusion.8), channel_id=1, source_target_pairs={{0,16},{4,20},{8,24},{12,28},{16,32},{20,36},{24,40},{28,44},{32,4... | collective-permute-start | bytes 1572872 | tf_op jit(solution)/shard_map/ppermute | solution.py:35
  35.5 24.6 %collective-permute-start.5 = (bf16[64,4096]{1,0:T(8,128)(2,1)S(1)}, bf16[64,4096]{1,0:T(8,128)(2,1)S(1)}, u32[]{:S(2)}, u32[]{:S(2)}) collective-permute-start(bf16[64,4096]{1,0:T(8,128)(2,1)S(1)} %pad_maximum_fusion.3), channel_id=1, source_target_pairs={{0,8},{4,12},{8,0},{12,4},{16,24},{20,28},{24,16},{28,20},{32,40},... | collective-permute-start | bytes 1572872 | tf_op jit(solution)/shard_map/ppermute | solution.py:35
  38.4 24.0 %collective-permute-start.4 = (bf16[64,4096]{1,0:T(8,128)(2,1)S(1)}, bf16[64,4096]{1,0:T(8,128)(2,1)S(1)}, u32[]{:S(2)}, u32[]{:S(2)}) collective-permute-start(bf16[64,4096]{1,0:T(8,128)(2,1)S(1)} %pad_maximum_fusion.3), channel_id=1, source_target_pairs={{0,12},{4,8},{8,4},{12,0},{16,28},{20,24},{24,20},{28,16},{32,44},... | collective-permute-start | bytes 1572872 | tf_op jit(solution)/shard_map/ppermute | solution.py:35
  39.3 20.9 %collective-permute-start.3 = (bf16[64,4096]{1,0:T(8,128)(2,1)S(1)}, bf16[64,4096]{1,0:T(8,128)(2,1)S(1)}, u32[]{:S(2)}, u32[]{:S(2)}) collective-permute-start(bf16[64,4096]{1,0:T(8,128)(2,1)S(1)} %pad_maximum_fusion.2.refs_0_), channel_id=1, source_target_pairs={{0,4},{4,0},{8,12},{12,8},{16,20},{20,16},{24,28},{28,24},{32,36},... | collective-permute-start | bytes 1572872 | tf_op jit(solution)/shard_map/ppermute | solution.py:35
  39.4 25.5 %collective-permute-start.6 = (bf16[64,4096]{1,0:T(8,128)(2,1)S(1)}, bf16[64,4096]{1,0:T(8,128)(2,1)S(1)}, u32[]{:S(2)}, u32[]{:S(2)}) collective-permute-start(bf16[64,4096]{1,0:T(8,128)(2,1)S(1)} %convolution_convert_fusion.6), channel_id=1, source_target_pairs={{0,32},{4,36},{8,40},{12,44},{16,48},{20,52},{24,56},{28,60},{32,6... | collective-permute-start | bytes 1572872 | tf_op jit(solution)/shard_map/ppermute | solution.py:35
  39.5 25.4 %collective-permute-start.7 = (bf16[64,4096]{1,0:T(8,128)(2,1)S(1)}, bf16[64,4096]{1,0:T(8,128)(2,1)S(1)}, u32[]{:S(2)}, u32[]{:S(2)}) collective-permute-start(bf16[64,4096]{1,0:T(8,128)(2,1)S(1)} %convolution_convert_fusion.5), channel_id=1, source_target_pairs={{0,96},{4,100},{8,104},{12,108},{16,112},{20,116},{24,120},{28,124... | collective-permute-start | bytes 1572872 | tf_op jit(solution)/shard_map/ppermute | solution.py:35
  65.1 40.0 %collective-permute-start.10 = (bf16[96,4096]{1,0:T(8,128)(2,1)S(1)}, bf16[96,4096]{1,0:T(8,128)(2,1)S(1)}, u32[]{:S(2)}, u32[]{:S(2)}) collective-permute-start(bf16[96,4096]{1,0:T(8,128)(2,1)S(1)} %get-tuple-element.203), channel_id=1, source_target_pairs={{0,8},{4,12},{8,0},{12,4},{16,24},{20,28},{24,16},{28,20},{32,40},... | collective-permute-start | bytes 2359304 | tf_op jit(solution)/shard_map/ppermute | solution.py:35
  68.0 37.1 %collective-permute-start.9 = (bf16[96,4096]{1,0:T(8,128)(2,1)S(1)}, bf16[96,4096]{1,0:T(8,128)(2,1)S(1)}, u32[]{:S(2)}, u32[]{:S(2)}) collective-permute-start(bf16[96,4096]{1,0:T(8,128)(2,1)S(1)} %get-tuple-element.203), channel_id=1, source_target_pairs={{0,12},{4,8},{8,4},{12,0},{16,28},{20,24},{24,20},{28,16},{32,44},... | collective-permute-start | bytes 2359304 | tf_op jit(solution)/shard_map/ppermute | solution.py:35
  68.9 36.2 %collective-permute-start.8 = (bf16[96,4096]{1,0:T(8,128)(2,1)S(1)}, bf16[96,4096]{1,0:T(8,128)(2,1)S(1)}, u32[]{:S(2)}, u32[]{:S(2)}) collective-permute-start(bf16[96,4096]{1,0:T(8,128)(2,1)S(1)} %get-tuple-element.105.refs_1_), channel_id=1, source_target_pairs={{0,4},{4,0},{8,12},{12,8},{16,20},{20,16},{24,28},{28,24},{32,36},... | collective-permute-start | bytes 2359304 | tf_op jit(solution)/shard_map/ppermute | solution.py:35
  68.9 36.2 %collective-permute-start.11 = (bf16[64,4096]{1,0:T(8,128)(2,1)S(1)}, bf16[64,4096]{1,0:T(8,128)(2,1)S(1)}, u32[]{:S(2)}, u32[]{:S(2)}) collective-permute-start(bf16[64,4096]{1,0:T(8,128)(2,1)S(1)} %convolution_convert_fusion.4), channel_id=1, source_target_pairs={{0,48},{4,52},{8,56},{12,60},{16,64},{20,68},{24,72},{28,76},{32,8... | collective-permute-start | bytes 1572872 | tf_op jit(solution)/shard_map/ppermute | solution.py:35
  68.9 36.2 %collective-permute-start.12 = (bf16[64,4096]{1,0:T(8,128)(2,1)S(1)}, bf16[64,4096]{1,0:T(8,128)(2,1)S(1)}, u32[]{:S(2)}, u32[]{:S(2)}) collective-permute-start(bf16[64,4096]{1,0:T(8,128)(2,1)S(1)} %convolution_convert_fusion.3), channel_id=1, source_target_pairs={{0,80},{4,84},{8,88},{12,92},{16,96},{20,100},{24,104},{28,108},{3... | collective-permute-start | bytes 1572872 | tf_op jit(solution)/shard_map/ppermute | solution.py:35
  106.2 18.7 %collective-permute-start.13 = (bf16[64,4096]{1,0:T(8,128)(2,1)S(1)}, bf16[64,4096]{1,0:T(8,128)(2,1)S(1)}, u32[]{:S(2)}, u32[]{:S(2)}) collective-permute-start(bf16[64,4096]{1,0:T(8,128)(2,1)S(1)} %pad_maximum_fusion.4.refs_0_), channel_id=1, source_target_pairs={{0,4},{4,0},{8,12},{12,8},{16,20},{20,16},{24,28},{28,24},{32,36},... | collective-permute-start | bytes 1572872 | tf_op jit(solution)/shard_map/ppermute | solution.py:35
  108.6 22.1 %collective-permute-start.15 = (bf16[64,4096]{1,0:T(8,128)(2,1)}, bf16[64,4096]{1,0:T(8,128)(2,1)}, u32[]{:S(2)}, u32[]{:S(2)}) collective-permute-start(bf16[64,4096]{1,0:T(8,128)(2,1)} %pad_maximum_fusion.5), channel_id=1, source_target_pairs={{0,8},{4,12},{8,0},{12,4},{16,24},{20,28},{24,16},{28,20},{32,40},... | collective-permute-start | bytes 1572872 | tf_op jit(solution)/shard_map/ppermute | solution.py:35
  110.2 23.6 %collective-permute-start.14 = (bf16[64,4096]{1,0:T(8,128)(2,1)}, bf16[64,4096]{1,0:T(8,128)(2,1)S(1)}, u32[]{:S(2)}, u32[]{:S(2)}) collective-permute-start(bf16[64,4096]{1,0:T(8,128)(2,1)} %pad_maximum_fusion.5), channel_id=1, source_target_pairs={{0,12},{4,8},{8,4},{12,0},{16,28},{20,24},{24,20},{28,16},{32,44},... | collective-permute-start | bytes 1572872 | tf_op jit(solution)/shard_map/ppermute | solution.py:35
  111.1 22.7 %collective-permute-start.16 = (bf16[64,4096]{1,0:T(8,128)(2,1)}, bf16[64,4096]{1,0:T(8,128)(2,1)S(1)}, u32[]{:S(2)}, u32[]{:S(2)}) collective-permute-start(bf16[64,4096]{1,0:T(8,128)(2,1)} %convolution_convert_fusion.2), channel_id=1, source_target_pairs={{0,64},{4,68},{8,72},{12,76},{16,80},{20,84},{24,88},{28,92},{32,9... | collective-permute-start | bytes 1572872 | tf_op jit(solution)/shard_map/ppermute | solution.py:35
  133.9 10.2 %collective-permute-start.17 = (bf16[32,4096]{1,0:T(8,128)(2,1)S(1)}, bf16[32,4096]{1,0:T(8,128)(2,1)S(1)}, u32[]{:S(2)}, u32[]{:S(2)}) collective-permute-start(bf16[32,4096]{1,0:T(8,128)(2,1)S(1)} %pad_maximum_fusion.6.refs_1_), channel_id=1, source_target_pairs={{0,4},{4,0},{8,12},{12,8},{16,20},{20,16},{24,28},{28,24},{32,36},... | collective-permute-start | bytes 786440 | tf_op jit(solution)/shard_map/ppermute | solution.py:35
  134.0 10.6 %collective-permute-start.19 = (bf16[32,4096]{1,0:T(8,128)(2,1)S(1)}, bf16[32,4096]{1,0:T(8,128)(2,1)S(1)}, u32[]{:S(2)}, u32[]{:S(2)}) collective-permute-start(bf16[32,4096]{1,0:T(8,128)(2,1)S(1)} %pad_maximum_fusion.7), channel_id=1, source_target_pairs={{0,8},{4,12},{8,0},{12,4},{16,24},{20,28},{24,16},{28,20},{32,40},... | collective-permute-start | bytes 786440 | tf_op jit(solution)/shard_map/ppermute | solution.py:35
  136.3 13.4 %collective-permute-start.18 = (bf16[32,4096]{1,0:T(8,128)(2,1)S(1)}, bf16[32,4096]{1,0:T(8,128)(2,1)S(1)}, u32[]{:S(2)}, u32[]{:S(2)}) collective-permute-start(bf16[32,4096]{1,0:T(8,128)(2,1)S(1)} %pad_maximum_fusion.7), channel_id=1, source_target_pairs={{0,12},{4,8},{8,4},{12,0},{16,28},{20,24},{24,20},{28,16},{32,44},... | collective-permute-start | bytes 786440 | tf_op jit(solution)/shard_map/ppermute | solution.py:35
  170.7 14.1 %collective-permute-start.20 = (bf16[80,4096]{1,0:T(8,128)(2,1)S(1)}, bf16[80,4096]{1,0:T(8,128)(2,1)S(1)}, u32[]{:S(2)}, u32[]{:S(2)}) collective-permute-start(bf16[80,4096]{1,0:T(8,128)(2,1)S(1)} %copy-done.24), channel_id=1, source_target_pairs={{0,4},{4,0},{8,12},{12,8},{16,20},{20,16},{24,28},{28,24},{32,36},... | collective-permute-start | bytes 1966088 | tf_op jit(solution)/shard_map/ppermute | solution.py:35
  170.9 15.3 %collective-permute-start.21 = (bf16[80,4096]{1,0:T(8,128)(2,1)S(1)}, bf16[80,4096]{1,0:T(8,128)(2,1)S(1)}, u32[]{:S(2)}, u32[]{:S(2)}) collective-permute-start(bf16[80,4096]{1,0:T(8,128)(2,1)S(1)} %copy-done.23), channel_id=1, source_target_pairs={{0,12},{4,8},{8,4},{12,0},{16,28},{20,24},{24,20},{28,16},{32,44},... | collective-permute-start | bytes 1966088 | tf_op jit(solution)/shard_map/ppermute | solution.py:35
  172.6 27.6 %collective-permute-start.22 = (bf16[80,4096]{1,0:T(8,128)(2,1)S(1)}, bf16[80,4096]{1,0:T(8,128)(2,1)S(1)}, u32[]{:S(2)}, u32[]{:S(2)}) collective-permute-start(bf16[80,4096]{1,0:T(8,128)(2,1)S(1)} %copy-done.22), channel_id=1, source_target_pairs={{0,8},{4,12},{8,0},{12,4},{16,24},{20,28},{24,16},{28,20},{32,40},... | collective-permute-start | bytes 1966088 | tf_op jit(solution)/shard_map/ppermute | solution.py:35
  200.2 38.6 %collective-permute-start.23 = (bf16[48,4096]{1,0:T(8,128)(2,1)}, bf16[48,4096]{1,0:T(8,128)(2,1)S(1)}, u32[]{:S(2)}, u32[]{:S(2)}) collective-permute-start(bf16[48,4096]{1,0:T(8,128)(2,1)} %get-tuple-element.157), channel_id=1, source_target_pairs={{0,4},{4,0},{8,12},{12,8},{16,20},{20,16},{24,28},{28,24},{32,36},... | collective-permute-start | bytes 1179656 | tf_op jit(solution)/shard_map/ppermute | solution.py:35
  200.2 38.6 %collective-permute-start.24 = (bf16[48,4096]{1,0:T(8,128)(2,1)}, bf16[48,4096]{1,0:T(8,128)(2,1)S(1)}, u32[]{:S(2)}, u32[]{:S(2)}) collective-permute-start(bf16[48,4096]{1,0:T(8,128)(2,1)} %get-tuple-element.158), channel_id=1, source_target_pairs={{0,12},{4,8},{8,4},{12,0},{16,28},{20,24},{24,20},{28,16},{32,44},... | collective-permute-start | bytes 1179656 | tf_op jit(solution)/shard_map/ppermute | solution.py:35
  201.3 37.5 %collective-permute-start.25 = (bf16[48,4096]{1,0:T(8,128)(2,1)}, bf16[48,4096]{1,0:T(8,128)(2,1)S(1)}, u32[]{:S(2)}, u32[]{:S(2)}) collective-permute-start(bf16[48,4096]{1,0:T(8,128)(2,1)} %get-tuple-element.159), channel_id=1, source_target_pairs={{0,8},{4,12},{8,0},{12,4},{16,24},{20,28},{24,16},{28,20},{32,40},... | collective-permute-start | bytes 1179656 | tf_op jit(solution)/shard_map/ppermute | solution.py:35
  203.9 23.0 %collective-permute-start.26 = (bf16[32,4096]{1,0:T(8,128)(2,1)S(1)}, bf16[32,4096]{1,0:T(8,128)(2,1)S(1)}, u32[]{:S(2)}, u32[]{:S(2)}) collective-permute-start(bf16[32,4096]{1,0:T(8,128)(2,1)S(1)} %pad_maximum_fusion.8), channel_id=1, source_target_pairs={{0,224},{4,228},{8,232},{12,236},{16,240},{20,244},{24,248},{28,25... | collective-permute-start | bytes 786440 | tf_op jit(solution)/shard_map/ppermute | solution.py:277
  228.9 9.9 %collective-permute-start.29 = (bf16[32,4096]{1,0:T(8,128)(2,1)S(1)}, bf16[32,4096]{1,0:T(8,128)(2,1)S(1)}, u32[]{:S(2)}, u32[]{:S(2)}) collective-permute-start(bf16[32,4096]{1,0:T(8,128)(2,1)S(1)} %pad_maximum_fusion.11), channel_id=1, source_target_pairs={{0,144},{4,148},{8,152},{12,156},{16,160},{20,164},{24,168},{28,17... | collective-permute-start | bytes 786440 | tf_op jit(solution)/shard_map/ppermute | solution.py:277
  239.2 21.3 %collective-permute-start.31 = (bf16[32,4096]{1,0:T(8,128)(2,1)S(1)}, bf16[32,4096]{1,0:T(8,128)(2,1)S(1)}, u32[]{:S(2)}, u32[]{:S(2)}) collective-permute-start(bf16[32,4096]{1,0:T(8,128)(2,1)S(1)} %pad_maximum_fusion.13), channel_id=1, source_target_pairs={{0,208},{4,212},{8,216},{12,220},{16,224},{20,228},{24,232},{28,23... | collective-permute-start | bytes 786440 | tf_op jit(solution)/shard_map/ppermute | solution.py:277
  239.6 21.0 %collective-permute-start.32 = (bf16[32,4096]{1,0:T(8,128)(2,1)S(1)}, bf16[32,4096]{1,0:T(8,128)(2,1)S(1)}, u32[]{:S(2)}, u32[]{:S(2)}) collective-permute-start(bf16[32,4096]{1,0:T(8,128)(2,1)S(1)} %pad_maximum_fusion.14), channel_id=1, source_target_pairs={{0,192},{4,196},{8,200},{12,204},{16,208},{20,212},{24,216},{28,22... | collective-permute-start | bytes 786440 | tf_op jit(solution)/shard_map/ppermute | solution.py:277
  242.4 32.2 %collective-permute-start.33 = (bf16[32,4096]{1,0:T(8,128)(2,1)S(1)}, bf16[32,4096]{1,0:T(8,128)(2,1)S(1)}, u32[]{:S(2)}, u32[]{:S(2)}) collective-permute-start(bf16[32,4096]{1,0:T(8,128)(2,1)S(1)} %pad_maximum_fusion.15), channel_id=1, source_target_pairs={{0,176},{4,180},{8,184},{12,188},{16,192},{20,196},{24,200},{28,20... | collective-permute-start | bytes 786440 | tf_op jit(solution)/shard_map/ppermute | solution.py:277
  (29 other events, 307.9 us)
Sparse Core Ops, SparseCore 0:
  14.7 98.3 all-gather.1
  169.8 98.4 reduce-scatter.1
